TPU v7x, 512 devices: a whole 4x4x16 slice. The times are simulated.
512 devices in a mesh: replica: 64 (over x, z), fsdp: 8 (over y, core).
Axes of the slice: x: 4, y: 4, z: 16, core: 2. Of those that a mesh axis runs over, the one named last changes fastest.
Arguments:
- anchor: bfloat16 [64, 2, 256, 8192], P('replica', None, 'fsdp'), may hold values from -0.0625 to 0.0625
- local_params: bfloat16 [64, 2, 256, 8192], P('replica', None, 'fsdp'), as said below
- staleness: int32 [64], replicated, may hold values from 0 to 15
- master: float32 [2, 256, 8192], P(None, 'fsdp', 'replica'), may hold values from -0.0625 to 0.0625
- momentum: float32 [2, 256, 8192], P(None, 'fsdp', 'replica'), may hold values from -0.006 to 0.006
Outputs:
- new_global: bfloat16 [2, 256, 8192], P(None, 'fsdp')
- new_master: float32 [2, 256, 8192], P(None, 'fsdp', 'replica')
- new_momentum: float32 [2, 256, 8192], P(None, 'fsdp', 'replica')
Inputs may be any that keep to these rules, and one draw needn't show every extreme that they name: `local_params`: a replica's parameters after its inner steps.
All inputs are finite; a program needn't handle non-finite values.
Results may differ from a plain program's by a relative error of at most 0.0022.
Values may be sent and summed in bfloat16 or wider, within the bound.
No kernel may reach another device: no remote copies, remote signals or barrier semaphores. Data moves between devices by JAX's collectives and lax.ppermute only.
A program may use at most 64 MiB of HBM per device.

v0:
```python
import jax
import jax.numpy as jnp
from jax import lax
from jax.sharding import PartitionSpec as P

D = 8192
ROWS = 256


def shards(anchor, local_params, staleness, master, momentum):
    weights = 1.0 / jnp.sqrt(1.0 + staleness.astype(jnp.float32))
    total = jnp.sum(weights)
    position = lax.axis_index("replica")
    own_weight = lax.dynamic_slice_in_dim(weights, position, 1, 0)[0]
    delta = anchor[0].astype(jnp.float32) - local_params[0].astype(jnp.float32)
    term = lax.optimization_barrier((own_weight * delta).astype(jnp.bfloat16))
    summed = lax.psum_scatter(term.astype(jnp.float32), "replica", scatter_dimension=2, tiled=True)
    outer_grad = summed / total
    squares = jnp.sum(outer_grad * outer_grad)
    square_total = lax.psum(squares, ("replica", "fsdp"))
    norm_value = jnp.sqrt(square_total)
    limit = 0.001 * jnp.sqrt(jnp.float32(2 * ROWS * D))
    factor = jnp.minimum(jnp.float32(1.0), limit / (norm_value + 1e-06))
    clipped = outer_grad * factor
    new_momentum = 0.9 * momentum + clipped
    new_master = master - 0.7 * (clipped + 0.9 * new_momentum)
    new_global = lax.all_gather(new_master.astype(jnp.bfloat16), "replica", axis=2, tiled=True)
    return (new_global, new_master, new_momentum)


def solution(mesh):
    placed = (
        P("replica", None, "fsdp", None),
        P("replica", None, "fsdp", None),
        P(),
        P(None, "fsdp", "replica"),
        P(None, "fsdp", "replica"),
    )
    return jax.shard_map(
        shards,
        mesh=mesh,
        in_specs=placed,
        out_specs=(P(None, "fsdp", None), P(None, "fsdp", "replica"), P(None, "fsdp", "replica")),
        check_vma=False,
    )
```

profile of v0, /device:TPU:1, one launch (start us, length us, event | category | flops | bytes accessed | tf_op | source)
XLA Modules:
  0.0 943.8 jit_solution(5452438197037450805)
XLA Ops:
  7.2 0.0 reduce-scatter.2.cloned.1.call-start
  7.2 1.3 fusion.1
  8.5 0.6 dynamic_slice.3
  9.1 2.5 fusion
  11.6 0.0 copy-start
  11.6 0.0 copy-start.1
  11.6 1.5 convert_element_type.28
  13.1 0.0 reduce-scatter.2.cloned.1.call-update
  13.1 0.0 all-gather.2.cloned.1.call-start
  13.2 688.7 %reduce-scatter.2.cloned.1.call-done = f32[2,32,128]{2,1,0:T(8,128)} async-done(((f32[2,32,8192]{2,1,0:T(8,128)}), f32[2,32,128]{2,1,0:T(8,128)}) %reduce-scatter.2.cloned.1.call-update) | async-done | bytes 32784 | tf_op jit(solution)/shard_map/reduce_scatter | solution.py:17
  701.9 2.0 multiply_reduce_fusion
  703.9 112.9 %psum.7 = f32[]{:T(128)} all-reduce(f32[]{:T(128)} %multiply_reduce_fusion), channel_id=1, replica_groups=mesh['replica'=64,'fsdp'=8] {'replica','fsdp'}, use_global_device_ids=true, to_apply=%region_3.0 | all-reduce | flops 1 | bytes 8 | tf_op jit(solution)/shard_map/psum | solution.py:20
  817.6 0.0 copy-done
  817.6 0.0 copy-done.1
  817.6 2.0 fusion.2
  819.6 0.0 all-gather.2.cloned.1.call-update
  819.6 115.0 %all-gather.2.cloned.1.call-done = bf16[2,32,8192]{2,1,0:T(8,128)(2,1)} async-done(((bf16[2,32,128]{2,1,0:T(8,128)(2,1)}), bf16[2,32,8192]{2,1,0:T(8,128)(2,1)}) %all-gather.2.cloned.1.call-update) | async-done | bytes 1048592 | tf_op jit(solution)/shard_map/all_gather | solution.py:27
  934.7 2.3 copy.9
Async XLA Ops:
  7.2 694.7 %reduce-scatter.2.cloned.1.call-start = ((), (), s32[]{:S(2)}) async-start(), calls=%async_computation.1 | async-start | bytes 2129920 | tf_op jit(solution)/shard_map/reduce_scatter | solution.py:17
  11.6 806.0 %copy-start = (f32[2,32,128]{2,1,0:T(8,128)S(1)}, f32[2,32,128]{2,1,0:T(8,128)}, u32[]{:S(2)}) copy-start(f32[2,32,128]{2,1,0:T(8,128)} %param.8) | copy-start | bytes 98308
  11.6 806.0 %copy-start.1 = (f32[2,32,128]{2,1,0:T(8,128)S(1)}, f32[2,32,128]{2,1,0:T(8,128)}, u32[]{:S(2)}) copy-start(f32[2,32,128]{2,1,0:T(8,128)} %param.9) | copy-start | bytes 98308
  13.1 921.6 %all-gather.2.cloned.1.call-start = ((), (), s32[]{:S(2)}) async-start(), calls=%async_computation.2 | async-start | bytes 1064960 | tf_op jit(solution)/shard_map/all_gather | solution.py:27
Sparse Core Ops, SparseCore 0:
  13.2 688.6 reduce-scatter.1
  819.8 114.8 all-gather.1
where the time goes:
time: 954 us; the launch traced here: 944 us
  waiting for transfers between devices  804 us (84%)
  blocking collectives  113 us (12%)
  between operations  14.8 us (2%)
    reduce_scatter x1, waiting for transfers between devices, shards(): lax.psum_scatter(term.astype(jnp.float32), 'replica', scatter_dimension=2...  689 us
    all_gather x1, waiting for transfers between devices, shards(): lax.all_gather(new_master.astype(jnp.bfloat16), 'replica', axis=2, tiled=...  115 us
    psum x1, blocking collectives, shards(): square_total = lax.psum(squares, ('replica', 'fsdp'))  113 us
  transfers between devices with their start and end apart: 2, of which 2 were waited for; matrix products, arithmetic and copies ran while one was open for 0% of the time, Pallas kernels for 0%

commit v1 on v0

v1 whole, which is shorter than its diff:
```python
import jax
import jax.numpy as jnp
from jax import lax
from jax.sharding import Mesh, PartitionSpec as P

D = 8192
ROWS = 256


def exchange(blocks, axes):
    return lax.all_to_all(blocks, axes, 0, 0, tiled=True)


def copies(block, count):
    return jnp.broadcast_to(block[None], (count,) + block.shape)


def shards(anchor, local_params, staleness, master, momentum):
    weights = 1.0 / jnp.sqrt(1.0 + staleness.astype(jnp.float32))
    total = jnp.sum(weights)
    position = lax.axis_index(("x", "u", "v"))
    mine = lax.axis_index("u")
    own_weight = jnp.sum(jnp.where(jnp.arange(64) == position, weights, 0.0))
    base = master - (0.7 * 0.9 * 0.9) * momentum
    bases = lax.all_gather(base, ("u", "v"), axis=0).reshape(4, 4, 2, 32, 128)
    delta = anchor[0].astype(jnp.float32) - local_params[0].astype(jnp.float32)
    term = (own_weight * delta).astype(jnp.bfloat16)
    term = term.reshape(2, 32, 4, 4, 4, 128).transpose(2, 4, 3, 0, 1, 5).reshape(16, 4, 2, 32, 128)
    near = exchange(term, ("x", "v"))
    partial = jnp.sum(near.astype(jnp.float32), axis=0).astype(jnp.bfloat16)
    far = exchange(copies(partial, 4), "u")
    outer_grad = jnp.sum(far.astype(jnp.float32), axis=0) / total
    squares = jnp.sum(outer_grad * outer_grad)
    parts = exchange(jnp.broadcast_to(squares, (128, 1, 128)), ("x", "v", "y", "c"))
    grads = exchange(copies(outer_grad.astype(jnp.bfloat16), 4), "v")
    norm_value = jnp.sqrt(jnp.sum(parts, axis=0)[0, 0])
    limit = 0.001 * jnp.sqrt(jnp.float32(2 * ROWS * D))
    factor = jnp.minimum(jnp.float32(1.0), limit / (norm_value + 1e-06))
    clipped = lax.dynamic_index_in_dim(outer_grad, mine, 0, keepdims=False) * factor
    new_momentum = 0.9 * momentum + clipped
    new_master = master - 0.7 * (clipped + 0.9 * new_momentum)
    quarter = bases - (0.7 * 1.9 * factor) * grads.transpose(1, 0, 2, 3, 4).astype(jnp.float32)
    quarters = exchange(copies(quarter.astype(jnp.bfloat16), 4), "x")
    new_global = quarters.transpose(3, 4, 0, 1, 2, 5).reshape(2, 32, D)
    return (new_global, new_master, new_momentum)


def solution(mesh):
    split = Mesh(mesh.devices.reshape(4, 4, 4, 4, 2), ("x", "u", "v", "y", "c"))
    replica, fsdp = ("x", "u", "v"), ("y", "c")
    placed = (
        P(replica, None, fsdp, None),
        P(replica, None, fsdp, None),
        P(),
        P(None, fsdp, replica),
        P(None, fsdp, replica),
    )
    return jax.shard_map(
        shards,
        mesh=split,
        in_specs=placed,
        out_specs=(P(None, fsdp, None), P(None, fsdp, replica), P(None, fsdp, replica)),
        check_vma=False,
    )
```

time: 954 us -> 148 us (0.16)
  the two profiles are of different devices: /device:TPU:1 before, /device:TPU:2 now
where the time goes in v1:
time: 148 us
  blocking collectives  111 us (75%)
  starting transfers between devices  15.3 us (10%)
  waiting for transfers between devices  9 us (6%)
  local copies, waits for them, and re-layouts  6.22 us (4%)
  other arithmetic  6.05 us (4%)
    all_to_all x3, blocking collectives, exchange(): return lax.all_to_all(blocks, axes, 0, 0, tiled=True)  77.6 us
    all_gather x1, blocking collectives, shards(): bases = lax.all_gather(base, ('u', 'v'), axis=0).reshape(4, 4, 2, 32, 128)  33 us
    all_to_all x2, starting transfers between devices, exchange(): return lax.all_to_all(blocks, axes, 0, 0, tiled=True)  15.3 us
    all_to_all x2, waiting for transfers between devices, exchange(): return lax.all_to_all(blocks, axes, 0, 0, tiled=True)  9 us
  transfers between devices with their start and end apart: 2, of which 1 were waited for; matrix products, arithmetic and copies ran while one was open for 0% of the time, Pallas kernels for 0%

profile of v1, /device:TPU:2, one launch (start us, length us, event | category | flops | bytes accessed | tf_op | source)
XLA Modules:
  0.0 148.0 jit_solution(16920879606487884187)
XLA Ops:
  0.6 1.3 fusion.4
  1.9 2.5 %multiply_convert_fusion = bf16[1,2,32,8192]{3,2,1,0:T(8,128)(2,1)S(1)} fusion(bf16[1,2,32,8192]{3,2,1,0:T(8,128)(2,1)} %param.6, bf16[1,2,32,8192]{3,2,1,0:T(8,128)(2,1)} %param.5, f32[]{:T(128)} %get-tuple-element.4), kind=kLoop, calls=%fused_computation | loop fusion | flops 2621440 | bytes 3145732 | tf_op jit(solution)/shard_map/convert_element_type | solution.py:27
  4.4 0.8 convert_element_type.43
  5.2 0.7 copy.23
  5.9 33.9 %all_to_all.25 = bf16[16,4,2,32,128]{4,3,2,1,0:T(8,128)(2,1)S(1)} all-to-all(bf16[16,4,2,32,128]{4,3,2,1,0:T(8,128)(2,1)S(1)} %bitcast.23), channel_id=1, replica_groups=mesh['x'=4,'u'=4,'v'=4,'y'=4,'c'=2] {'x','v'}, dimensions={0} | all-to-all | bytes 2097152 | tf_op jit(solution)/shard_map/all_to_all | solution.py:11
  39.7 0.2 reduce_sum.60
  40.0 30.5 %all_to_all.26 = bf16[4,4,2,32,128]{4,3,2,1,0:T(8,128)(2,1)S(1)} all-to-all(bf16[4,4,2,32,128]{4,3,2,1,0:T(8,128)(2,1)S(1)} %broadcast_in_dim.13), channel_id=1, replica_groups=mesh['x'=4,'u'=4,'v'=4,'y'=4,'c'=2] {'u'}, dimensions={0} | all-to-all | bytes 524288 | tf_op jit(solution)/shard_map/all_to_all | solution.py:11
  70.5 0.0 copy-start
  70.5 0.0 copy-start.1
  70.5 1.3 multiply_reduce_fusion
  71.8 1.3 broadcast_in_dim.14
  73.1 11.8 %all-to-all-start.2 = ((f32[128,1,128]{2,1,0:T(1,128)}), f32[128,1,128]{2,1,0:T(1,128)S(1)}, u32[]{:S(2)}, u32[]{:S(2)}) async-start(f32[128,1,128]{2,1,0:T(1,128)} %broadcast_in_dim.14), calls=%async_computation.2 | async-start | bytes 131072 | tf_op jit(solution)/shard_map/all_to_all | solution.py:11
  85.0 9.0 %all-to-all-done.2 = f32[128,1,128]{2,1,0:T(1,128)S(1)} async-done(((f32[128,1,128]{2,1,0:T(1,128)}), f32[128,1,128]{2,1,0:T(1,128)S(1)}, u32[]{:S(2)}, u32[]{:S(2)}) %all-to-all-start.2) | async-done | bytes 65568 | tf_op jit(solution)/shard_map/all_to_all | solution.py:11
  94.0 0.8 broadcast_in_dim.28
  94.8 3.4 %all-to-all-start.3 = ((bf16[4,4,2,32,128]{4,3,2,1,0:T(8,128)(2,1)}), bf16[4,4,2,32,128]{4,3,2,1,0:T(8,128)(2,1)S(1)}, u32[]{:S(2)}, u32[]{:S(2)}) async-start(bf16[4,4,2,32,128]{4,3,2,1,0:T(8,128)(2,1)} %broadcast_in_dim.28), calls=%async_computation.3 | async-start | bytes 524288 | tf_op jit(solution)/shard_map/all_to_all | solution.py:11
  98.3 0.0 copy-done
  98.3 0.0 copy-done.1
  98.4 0.6 fusion.2
  99.0 33.0 %all-gather = f32[32,32,128]{2,1,0:T(8,128)S(1)} all-gather(f32[2,32,128]{2,1,0:T(8,128)S(1)} %get-tuple-element.9), channel_id=2, replica_groups=mesh['x'=4,'u'=4,'v'=4,'y'=4,'c'=2] {'u','v'}, dimensions={0}, use_global_device_ids=true | all-gather | bytes 557056 | tf_op jit(solution)/shard_map/all_gather | solution.py:25
  132.0 0.0 all-to-all-done.3
  132.0 0.1 fusion
  132.1 0.2 copy.26
  132.3 0.3 broadcast_in_dim.29
  132.6 13.2 %all_to_all.27 = bf16[4,4,4,2,32,128]{5,2,1,4,3,0:T(4,128)(2,1)S(1)} all-to-all(bf16[4,4,4,2,32,128]{5,2,1,4,3,0:T(4,128)(2,1)S(1)} %broadcast_in_dim.29), channel_id=1, replica_groups=mesh['x'=4,'u'=4,'v'=4,'y'=4,'c'=2] {'x'}, dimensions={0} | all-to-all | bytes 2097152 | tf_op jit(solution)/shard_map/all_to_all | solution.py:11
  145.8 0.6 copy.27
  146.4 1.6 %reshape.42 = bf16[2,32,8192]{2,1,0:T(8,128)(2,1)} reshape(bf16[2,32,4,4,4,128]{5,4,3,2,1,0:T(4,128)(2,1)S(1)} %copy.27) | data formatting | bytes 2097152 | tf_op jit(solution)/shard_map/reshape | solution.py:44
  (4 shorter events, 0.1 us)
Async XLA Ops:
  70.5 27.8 %copy-start = (f32[2,32,128]{2,1,0:T(8,128)S(1)}, f32[2,32,128]{2,1,0:T(8,128)}, u32[]{:S(2)}) copy-start(f32[2,32,128]{2,1,0:T(8,128)} %param.8) | copy-start | bytes 98308
  70.5 27.8 %copy-start.1 = (f32[2,32,128]{2,1,0:T(8,128)S(1)}, f32[2,32,128]{2,1,0:T(8,128)}, u32[]{:S(2)}) copy-start(f32[2,32,128]{2,1,0:T(8,128)} %param.9) | copy-start | bytes 98308
  73.1 20.9 %all-to-all-start.2 = ((f32[128,1,128]{2,1,0:T(1,128)}), f32[128,1,128]{2,1,0:T(1,128)S(1)}, u32[]{:S(2)}, u32[]{:S(2)}) async-start(f32[128,1,128]{2,1,0:T(1,128)} %broadcast_in_dim.14), calls=%async_computation.2 | async-start | bytes 131072 | tf_op jit(solution)/shard_map/all_to_all | solution.py:11
  94.8 37.2 %all-to-all-start.3 = ((bf16[4,4,2,32,128]{4,3,2,1,0:T(8,128)(2,1)}), bf16[4,4,2,32,128]{4,3,2,1,0:T(8,128)(2,1)S(1)}, u32[]{:S(2)}, u32[]{:S(2)}) async-start(bf16[4,4,2,32,128]{4,3,2,1,0:T(8,128)(2,1)} %broadcast_in_dim.28), calls=%async_computation.3 | async-start | bytes 524288 | tf_op jit(solution)/shard_map/all_to_all | solution.py:11

commit v2 on v1

v2 whole, which is shorter than its diff:
```python
import jax
import jax.numpy as jnp
from jax import lax
from jax.experimental import pallas as pl
from jax.experimental.pallas import tpu as pltpu
from jax.sharding import Mesh, PartitionSpec as P

D = 8192
ROWS = 256
LEVELS = 32000.0
VMEM = pl.BlockSpec(memory_space=pltpu.VMEM)
SMEM = pl.BlockSpec(memory_space=pltpu.SMEM)
PARAMS = pltpu.CompilerParams(vmem_limit_bytes=6 * 2**20)


def exchange(blocks, axes):
    return lax.all_to_all(blocks, axes, 0, 0, tiled=True)


def copies(block, count):
    return jnp.broadcast_to(block[None], (count,) + block.shape)


def weights_of(staleness_ref):
    return 1.0 / jnp.sqrt(1.0 + staleness_ref[...].astype(jnp.float32))


def encode(values):
    largest = jnp.max(jnp.abs(values), axis=0, keepdims=True)
    exponent = jnp.clip(jnp.floor(jnp.log2(largest) + 0.002) + 1.0, -126.0, 128.0)
    half = jnp.exp2(-0.5 * exponent)
    coded = jnp.round(values * half * half * LEVELS)
    return coded.astype(jnp.int32).astype(jnp.int16), exponent


def pack_exponents(exponents):
    rows = jnp.concatenate(exponents + [jnp.zeros((12, 128), jnp.float32)], axis=0)
    return rows.astype(jnp.int32).astype(jnp.int16)


def widen(coded):
    return coded.astype(jnp.int32).astype(jnp.float32)


def decode_sum(ref, block):
    result = None
    for sender in range(4):
        exponent = widen(ref[sender, 256:272, :])[block : block + 1]
        half = jnp.exp2(0.5 * exponent)
        part = widen(ref[sender, 64 * block : 64 * block + 64, :]) * (half * (1.0 / LEVELS)) * half
        result = part if result is None else result + part
    return result


def term_kernel(position_ref, staleness_ref, anchor_ref, local_ref, term_ref):
    weights = weights_of(staleness_ref)
    lane = lax.broadcasted_iota(jnp.int32, (1, 64), 1)
    own = jnp.sum(jnp.where(lane == position_ref[0], weights, 0.0), axis=1, keepdims=True)
    for half in range(2):
        delta = anchor_ref[0, half].astype(jnp.float32) - local_ref[0, half].astype(jnp.float32)
        term_ref[0, half] = (own * delta).astype(jnp.bfloat16)


def near_kernel(near_ref, coded_ref):
    for v in range(4):
        exponents = []
        for u in range(4):
            column = (4 * u + v) * 128
            total = near_ref[0, :, :, column : column + 128].astype(jnp.float32)
            for sender in range(1, 4):
                total = total + near_ref[sender, :, :, column : column + 128].astype(jnp.float32)
            coded_ref[v, 64 * u : 64 * u + 64, :], exponent = encode(total.reshape(64, 128))
            exponents.append(exponent)
        coded_ref[v, 256:272, :] = pack_exponents(exponents)


def far_kernel(coded_ref, master_ref, momentum_ref, out_ref):
    exponents = []
    for u in range(4):
        out_ref[64 * u : 64 * u + 64, :], exponent = encode(decode_sum(coded_ref, u))
        exponents.append(exponent)
    out_ref[256:272, :] = pack_exponents(exponents)
    base = master_ref[...] - (0.7 * 0.9 * 0.9) * momentum_ref[...]
    fixed = jnp.round(base.reshape(64, 128) * 2.0**34).astype(jnp.int32)
    out_ref[272:336, :] = (fixed >> 16).astype(jnp.int16)
    out_ref[336:400, :] = ((fixed & 65535) - 32768).astype(jnp.int16)


def grad_kernel(staleness_ref, far_ref, grad_ref, squares_ref):
    total = jnp.sum(weights_of(staleness_ref), axis=1, keepdims=True)
    squares = jnp.zeros((64, 128), jnp.float32)
    for u in range(4):
        grad = decode_sum(far_ref, u) / total
        grad_ref[u] = grad
        squares = squares + grad * grad
    squares = jnp.sum(jnp.sum(squares, axis=0, keepdims=True), axis=1, keepdims=True)
    squares_ref[...] = jnp.broadcast_to(squares[None], (128, 1, 128))


def update_kernel(mine_ref, parts_ref, grad_ref, far_ref, master_ref, momentum_ref, blocks_ref, new_master_ref, new_momentum_ref):
    norm = jnp.sqrt(jnp.sum(parts_ref[...], axis=0))
    limit = 0.001 * float(2 * ROWS * D) ** 0.5
    factor = jnp.minimum(1.0, limit / (norm + 1e-06))
    for u in range(4):
        high = far_ref[u, 272:336, :].astype(jnp.int32)
        low = far_ref[u, 336:400, :].astype(jnp.int32)
        base = (high * 65536 + (low + 32768)).astype(jnp.float32) * 2.0**-34
        blocks_ref[u] = (base - (0.7 * 1.9) * (grad_ref[u] * factor)).astype(jnp.bfloat16)
    clipped = (grad_ref[mine_ref[0]] * factor).reshape(2, 32, 128)
    new_momentum = 0.9 * momentum_ref[...] + clipped
    new_momentum_ref[...] = new_momentum
    new_master_ref[...] = master_ref[...] - 0.7 * (clipped + 0.9 * new_momentum)


def place_kernel(blocks_ref, out_ref):
    for v in range(4):
        for u in range(4):
            column = (4 * u + v) * 128
            out_ref[:, :, column : column + 128] = blocks_ref[0, v, u].reshape(2, 32, 128)


def shards(anchor, local_params, staleness, master, momentum):
    position = lax.axis_index(("x", "u", "v")).astype(jnp.int32).reshape(1)
    mine = lax.axis_index("u").astype(jnp.int32).reshape(1)
    staleness = staleness.reshape(1, 64)
    f32, bf16, i16 = jnp.float32, jnp.bfloat16, jnp.int16
    term = pl.pallas_call(
        term_kernel,
        grid=(4,),
        out_shape=jax.ShapeDtypeStruct((4, 2, 32, 2048), bf16),
        in_specs=[
            SMEM,
            pl.BlockSpec((1, 64), lambda i: (0, 0)),
            pl.BlockSpec((1, 2, 32, 2048), lambda i: (0, 0, 0, i)),
            pl.BlockSpec((1, 2, 32, 2048), lambda i: (0, 0, 0, i)),
        ],
        out_specs=pl.BlockSpec((1, 2, 32, 2048), lambda i: (i, 0, 0, 0)),
        name="term", compiler_params=PARAMS,
    )(position, staleness, anchor, local_params)
    near = exchange(term, "x")
    coded = pl.pallas_call(
        near_kernel, out_shape=jax.ShapeDtypeStruct((4, 272, 128), i16), in_specs=[VMEM], out_specs=VMEM, name="near", compiler_params=PARAMS,
    )(near)
    coded = exchange(coded, "v")
    packed = pl.pallas_call(
        far_kernel, out_shape=jax.ShapeDtypeStruct((400, 128), i16), in_specs=[VMEM] * 3, out_specs=VMEM, name="far", compiler_params=PARAMS,
    )(coded, master, momentum)
    far = exchange(copies(packed, 4), "u")
    grad, squares = pl.pallas_call(
        grad_kernel,
        out_shape=(jax.ShapeDtypeStruct((4, 64, 128), f32), jax.ShapeDtypeStruct((128, 1, 128), f32)),
        in_specs=[VMEM] * 2,
        out_specs=(VMEM, VMEM),
        name="grad", compiler_params=PARAMS,
    )(staleness, far)
    parts = exchange(squares, ("x", "v", "y", "c"))
    block = jax.ShapeDtypeStruct((2, 32, 128), f32)
    blocks, new_master, new_momentum = pl.pallas_call(
        update_kernel,
        out_shape=(jax.ShapeDtypeStruct((4, 64, 128), bf16), block, block),
        in_specs=[SMEM] + [VMEM] * 5,
        out_specs=(VMEM, VMEM, VMEM),
        name="update", compiler_params=PARAMS,
    )(mine, parts, grad, far, master, momentum)
    quarter = exchange(copies(blocks, 4), "v")
    quarters = exchange(copies(quarter, 4), "x")
    new_global = pl.pallas_call(
        place_kernel,
        grid=(4,),
        out_shape=jax.ShapeDtypeStruct((2, 32, D), bf16),
        in_specs=[pl.BlockSpec((1, 4, 4, 64, 128), lambda i: (i, 0, 0, 0, 0))],
        out_specs=pl.BlockSpec((2, 32, 2048), lambda i: (0, 0, i)),
        name="place", compiler_params=PARAMS,
    )(quarters)
    return (new_global, new_master, new_momentum)


def solution(mesh):
    split = Mesh(mesh.devices.reshape(4, 4, 4, 4, 2), ("x", "u", "v", "y", "c"))
    replica, fsdp = ("x", "u", "v"), ("y", "c")
    placed = (
        P(replica, None, fsdp, None),
        P(replica, None, fsdp, None),
        P(),
        P(None, fsdp, replica),
        P(None, fsdp, replica),
    )
    return jax.shard_map(
        shards,
        mesh=split,
        in_specs=placed,
        out_specs=(P(None, fsdp, None), P(None, fsdp, replica), P(None, fsdp, replica)),
        check_vma=False,
    )
```

time: 148 us -> 123 us (0.83)
  the two profiles are of different devices: /device:TPU:2 before, /device:TPU:1 now
where the time goes in v2:
time: 123 us; the launch traced here: 121 us
  blocking collectives  113 us (92%)
  Pallas kernels  3.77 us (3%)
  local copies, waits for them, and re-layouts  3.45 us (3%)
    all_to_all x6, blocking collectives, exchange(): return lax.all_to_all(blocks, axes, 0, 0, tiled=True)  113 us
    unnamed x10, local copies, waits for them, and re-layouts  3.11 us

profile of v2, /device:TPU:1, one launch (start us, length us, event | category | flops | bytes accessed | tf_op | source)
XLA Modules:
  0.0 121.1 jit_solution(9787207970535249814)
XLA Ops:
  0.6 0.0 copy-start.4
  0.7 0.6 copy-done.4
  1.3 0.0 copy-start
  1.3 1.2 %copy-done = bf16[1,2,32,8192]{3,2,1,0:T(8,128)(2,1)S(1)} copy-done((bf16[1,2,32,8192]{3,2,1,0:T(8,128)(2,1)S(1)}, bf16[1,2,32,8192]{3,2,1,0:T(8,128)(2,1)}, u32[]{:S(2)}) %copy-start) | copy-done | bytes 1048600
  2.5 0.0 copy-start.1
  2.5 1.2 %copy-done.1 = bf16[1,2,32,8192]{3,2,1,0:T(8,128)(2,1)S(1)} copy-done((bf16[1,2,32,8192]{3,2,1,0:T(8,128)(2,1)S(1)}, bf16[1,2,32,8192]{3,2,1,0:T(8,128)(2,1)}, u32[]{:S(2)}) %copy-start.1) | copy-done | bytes 1048600
  3.7 0.7 term.1
  4.5 15.1 %all_to_all.30.near_ref = bf16[4,2,32,2048]{3,2,1,0:T(8,128)(2,1)S(1)} all-to-all(bf16[4,2,32,2048]{3,2,1,0:T(8,128)(2,1)S(1)} %term.1), channel_id=1, replica_groups=mesh['x'=4,'u'=4,'v'=4,'y'=4,'c'=2] {'x'}, dimensions={0} | all-to-all | bytes 2097152 | tf_op jit(solution)/shard_map/all_to_all | solution.py:17
  19.6 0.3 near.1
  19.9 0.0 copy-start.2
  19.9 0.0 copy-start.3
  19.9 15.7 %all_to_all.31.coded_ref = s16[4,272,128]{2,1,0:T(8,128)(2,1)S(1)} all-to-all(s16[4,272,128]{2,1,0:T(8,128)(2,1)S(1)} %near.1), channel_id=1, replica_groups=mesh['x'=4,'u'=4,'v'=4,'y'=4,'c'=2] {'v'}, dimensions={0} | all-to-all | bytes 557056 | tf_op jit(solution)/shard_map/all_to_all | solution.py:17
  35.6 0.0 copy-done.2
  35.6 0.0 copy-done.3
  35.6 0.1 far.1
  35.8 0.1 broadcast_in_dim.6
  35.9 34.2 %all_to_all.32.far_ref = s16[4,400,128]{2,1,0:T(8,128)(2,1)S(1)} all-to-all(s16[4,400,128]{2,1,0:T(8,128)(2,1)S(1)} %broadcast_in_dim.6), channel_id=1, replica_groups=mesh['x'=4,'u'=4,'v'=4,'y'=4,'c'=2] {'u'}, dimensions={0} | all-to-all | bytes 819200 | tf_op jit(solution)/shard_map/all_to_all | solution.py:17
  70.0 0.2 grad.1
  70.3 24.3 %all_to_all.33.parts_ref = f32[128,1,128]{2,1,0:T(1,128)S(1)} all-to-all(f32[128,1,128]{2,1,0:T(1,128)S(1)} %get-tuple-element.8), channel_id=1, replica_groups=mesh['x'=4,'u'=4,'v'=4,'y'=4,'c'=2] {'x','v','y','c'}, dimensions={0} | all-to-all | bytes 131072 | tf_op jit(solution)/shard_map/all_to_all | solution.py:17
  94.6 0.8 update.1
  95.4 9.3 %all_to_all.34 = bf16[4,4,64,128]{3,2,1,0:T(8,128)(2,1)S(1)} all-to-all(bf16[4,4,64,128]{3,2,1,0:T(8,128)(2,1)S(1)} %broadcast_in_dim.7), channel_id=1, replica_groups=mesh['x'=4,'u'=4,'v'=4,'y'=4,'c'=2] {'v'}, dimensions={0} | all-to-all | bytes 524288 | tf_op jit(solution)/shard_map/all_to_all | solution.py:17
  104.7 0.2 broadcast_in_dim.8
  105.0 14.6 %all_to_all.35.blocks_ref = bf16[4,4,4,64,128]{4,3,2,1,0:T(8,128)(2,1)S(1)} all-to-all(bf16[4,4,4,64,128]{4,3,2,1,0:T(8,128)(2,1)S(1)} %broadcast_in_dim.8), channel_id=1, replica_groups=mesh['x'=4,'u'=4,'v'=4,'y'=4,'c'=2] {'x'}, dimensions={0} | all-to-all | bytes 2097152 | tf_op jit(solution)/shard_map/all_to_all | solution.py:17
  119.5 1.6 %place.1 = bf16[2,32,8192]{2,1,0:T(8,128)(2,1)} custom-call(bf16[4,4,4,64,128]{4,3,2,1,0:T(8,128)(2,1)S(1)} %all_to_all.35.blocks_ref), custom_call_target="tpu_custom_call" | custom-call | tf_op jit(solution)/shard_map/place/pallas_call | solution.py:167
  (1 shorter events, 0.0 us)
Async XLA Ops:
  0.6 0.7 copy-start.4
  1.3 1.2 %copy-start = (bf16[1,2,32,8192]{3,2,1,0:T(8,128)(2,1)S(1)}, bf16[1,2,32,8192]{3,2,1,0:T(8,128)(2,1)}, u32[]{:S(2)}) copy-start(bf16[1,2,32,8192]{3,2,1,0:T(8,128)(2,1)} %anchor_ref.1) | copy-start | bytes 3145732
  2.5 1.2 %copy-start.1 = (bf16[1,2,32,8192]{3,2,1,0:T(8,128)(2,1)S(1)}, bf16[1,2,32,8192]{3,2,1,0:T(8,128)(2,1)}, u32[]{:S(2)}) copy-start(bf16[1,2,32,8192]{3,2,1,0:T(8,128)(2,1)} %local_ref.1) | copy-start | bytes 3145732
  19.9 15.8 %copy-start.2 = (f32[2,32,128]{2,1,0:T(8,128)S(1)}, f32[2,32,128]{2,1,0:T(8,128)}, u32[]{:S(2)}) copy-start(f32[2,32,128]{2,1,0:T(8,128)} %master_ref.3) | copy-start | bytes 98308
  19.9 15.8 %copy-start.3 = (f32[2,32,128]{2,1,0:T(8,128)S(1)}, f32[2,32,128]{2,1,0:T(8,128)}, u32[]{:S(2)}) copy-start(f32[2,32,128]{2,1,0:T(8,128)} %momentum_ref.3) | copy-start | bytes 98308

commit v3 on v2

v3 whole, which is shorter than its diff:
```python
import jax
import jax.numpy as jnp
from jax import lax
from jax.experimental import pallas as pl
from jax.experimental.pallas import tpu as pltpu
from jax.sharding import Mesh, PartitionSpec as P

D = 8192
ROWS = 256
LEVELS = 32000.0
VMEM = pl.BlockSpec(memory_space=pltpu.VMEM)
SMEM = pl.BlockSpec(memory_space=pltpu.SMEM)
HBM = pl.BlockSpec(memory_space=pltpu.HBM)


def exchange(blocks, axes):
    return lax.all_to_all(blocks, axes, 0, 0, tiled=True)


def copies(block, count):
    return jnp.broadcast_to(block[None], (count,) + block.shape)


def encode(values):
    largest = jnp.max(jnp.abs(values), axis=0, keepdims=True)
    exponent = jnp.clip(jnp.floor(jnp.log2(largest) + 0.002) + 1.0, -126.0, 128.0)
    half = jnp.exp2(-0.5 * exponent)
    coded = jnp.round(values * half * half * LEVELS)
    return coded.astype(jnp.int32).astype(jnp.int16), exponent


def pack_exponents(exponents):
    rows = exponents + [jnp.zeros((16 - len(exponents), 128), jnp.float32)]
    return jnp.concatenate(rows, axis=0).astype(jnp.int32).astype(jnp.int16)


def widen(coded):
    return coded.astype(jnp.int32).astype(jnp.float32)


def decode(coded, exponent):
    half = jnp.exp2(0.5 * exponent)
    return widen(coded) * (half * (1.0 / LEVELS)) * half


def decode_sum(ref, block):
    result = None
    for sender in range(4):
        exponent = widen(ref[sender, 256:272, :])[block : block + 1]
        part = decode(ref[sender, 64 * block : 64 * block + 64, :], exponent)
        result = part if result is None else result + part
    return result


def term_kernel(position_ref, staleness_ref, anchor_ref, local_ref, term_ref, total_ref, stale, anchors, locals_, sems, stale_sem):
    first = pltpu.make_async_copy(staleness_ref, stale, stale_sem)
    first.start()
    pending = []
    for quarter in range(4):
        columns = pl.ds(2048 * quarter, 2048)
        pair = (
            pltpu.make_async_copy(anchor_ref.at[0, :, :, columns], anchors.at[quarter], sems.at[0, quarter]),
            pltpu.make_async_copy(local_ref.at[0, :, :, columns], locals_.at[quarter], sems.at[1, quarter]),
        )
        pair[0].start()
        pair[1].start()
        pending.append(pair)
    first.wait()
    weights = 1.0 / jnp.sqrt(1.0 + stale[...].astype(jnp.float32))
    lane = lax.broadcasted_iota(jnp.int32, (1, 64), 1)
    own = jnp.sum(jnp.where(lane == position_ref[0], weights, 0.0), axis=1, keepdims=True)
    total_ref[...] = jnp.broadcast_to(jnp.sum(weights, axis=1, keepdims=True), (8, 128))
    for quarter in range(4):
        pending[quarter][0].wait()
        pending[quarter][1].wait()
        for half in range(2):
            delta = anchors[quarter, half].astype(jnp.float32) - locals_[quarter, half].astype(jnp.float32)
            term_ref[quarter, half] = (own * delta).astype(jnp.bfloat16)


def near_kernel(near_ref, coded_ref):
    for v in range(4):
        exponents = []
        for u in range(4):
            column = (4 * u + v) * 128
            total = near_ref[0, :, :, column : column + 128].astype(jnp.float32)
            for sender in range(1, 4):
                total = total + near_ref[sender, :, :, column : column + 128].astype(jnp.float32)
            coded_ref[v, 64 * u : 64 * u + 64, :], exponent = encode(total.reshape(64, 128))
            exponents.append(exponent)
        coded_ref[v, 256:272, :] = pack_exponents(exponents)


def far_kernel(coded_ref, master_ref, momentum_ref, out_ref):
    exponents = []
    for u in range(4):
        out_ref[64 * u : 64 * u + 64, :], exponent = encode(decode_sum(coded_ref, u))
        exponents.append(exponent)
    base = master_ref[...] - (0.7 * 0.9 * 0.9) * momentum_ref[...]
    out_ref[272:336, :], exponent = encode(base.reshape(64, 128))
    out_ref[256:272, :] = pack_exponents(exponents + [exponent])


def grad_kernel(total_ref, far_ref, grad_ref, coded_ref):
    exponents, base_exponents = [], []
    for u in range(4):
        grad = decode_sum(far_ref, u) / total_ref[0:1, :]
        grad_ref[u] = grad
        coded_ref[64 * u : 64 * u + 64, :], exponent = encode(grad)
        exponents.append(exponent)
        coded_ref[272 + 64 * u : 336 + 64 * u, :] = far_ref[u, 272:336, :]
        base_exponents.append(widen(far_ref[u, 256:272, :])[4:5])
    coded_ref[256:272, :] = pack_exponents(exponents + base_exponents)


def grad_of(coded_ref, v, u):
    return decode(coded_ref[v, 64 * u : 64 * u + 64, :], widen(coded_ref[v, 256:272, :])[u : u + 1])


def base_of(coded_ref, v, u):
    return decode(coded_ref[v, 272 + 64 * u : 336 + 64 * u, :], widen(coded_ref[v, 256:272, :])[4 + u : 5 + u])


def squares_kernel(coded_ref, squares_ref):
    squares = jnp.zeros((64, 128), jnp.float32)
    for v in range(4):
        for u in range(4):
            grad = grad_of(coded_ref, v, u)
            squares = squares + grad * grad
    squares = jnp.sum(jnp.sum(squares, axis=0, keepdims=True), axis=1, keepdims=True)
    squares_ref[...] = jnp.broadcast_to(squares[None], (32, 1, 128))


def update_kernel(mine_ref, parts_ref, coded_ref, grad_ref, master_ref, momentum_ref, quarter_ref, new_master_ref, new_momentum_ref):
    norm = jnp.sqrt(jnp.sum(parts_ref[...], axis=0))
    limit = 0.001 * float(2 * ROWS * D) ** 0.5
    factor = jnp.minimum(1.0, limit / (norm + 1e-06))
    for v in range(4):
        for u in range(4):
            column = (4 * u + v) * 128
            value = base_of(coded_ref, v, u) - (0.7 * 1.9) * (grad_of(coded_ref, v, u) * factor)
            quarter_ref[:, :, column : column + 128] = value.astype(jnp.bfloat16).reshape(2, 32, 128)
    clipped = (grad_ref[mine_ref[0]] * factor).reshape(2, 32, 128)
    new_momentum = 0.9 * momentum_ref[...] + clipped
    new_momentum_ref[...] = new_momentum
    new_master_ref[...] = master_ref[...] - 0.7 * (clipped + 0.9 * new_momentum)


def place_kernel(quarters_ref, out_ref, sems):
    pending = []
    for quarter in range(4):
        copy = pltpu.make_async_copy(quarters_ref.at[quarter], out_ref.at[:, :, pl.ds(2048 * quarter, 2048)], sems.at[quarter])
        copy.start()
        pending.append(copy)
    for copy in pending:
        copy.wait()


def call(kernel, name, outs, in_specs, out_specs, scratch=(), mib=6):
    return pl.pallas_call(
        kernel,
        out_shape=[jax.ShapeDtypeStruct(shape, dtype) for shape, dtype in outs],
        in_specs=in_specs,
        out_specs=out_specs,
        scratch_shapes=scratch,
        name=name,
        compiler_params=pltpu.CompilerParams(vmem_limit_bytes=mib * 2**20),
    )


def shards(anchor, local_params, staleness, master, momentum):
    position = lax.axis_index(("x", "u", "v")).astype(jnp.int32).reshape(1)
    mine = lax.axis_index("u").astype(jnp.int32).reshape(1)
    f32, bf16, i16 = jnp.float32, jnp.bfloat16, jnp.int16
    held = pltpu.VMEM((4, 2, 32, 2048), bf16)
    dma = pltpu.SemaphoreType.DMA
    term, total = call(
        term_kernel,
        "term",
        [((4, 2, 32, 2048), bf16), ((8, 128), f32)],
        [SMEM, HBM, HBM, HBM],
        [VMEM, VMEM],
        [pltpu.VMEM((1, 64), jnp.int32), held, held, dma((2, 4)), dma(())],
        mib=56,
    )(position, staleness.reshape(1, 64), anchor, local_params)
    near = exchange(term, "x")
    (coded,) = call(near_kernel, "near", [((4, 272, 128), i16)], [VMEM], [VMEM])(near)
    coded = exchange(coded, "v")
    (packed,) = call(far_kernel, "far", [((336, 128), i16)], [VMEM] * 3, [VMEM])(coded, master, momentum)
    far = lax.all_gather(packed, "u", axis=0)
    grad, coded = call(
        grad_kernel, "grad", [((4, 64, 128), f32), ((528, 128), i16)], [VMEM] * 2, [VMEM] * 2
    )(total, far)
    coded = lax.all_gather(coded, "v", axis=0)
    (squares,) = call(squares_kernel, "squares", [((32, 1, 128), f32)], [VMEM], [VMEM])(coded)
    parts = exchange(squares, ("x", "y", "c"))
    quarter, new_master, new_momentum = call(
        update_kernel,
        "update",
        [((2, 32, 2048), bf16), ((2, 32, 128), f32), ((2, 32, 128), f32)],
        [SMEM] + [VMEM] * 5,
        [VMEM] * 3,
    )(mine, parts, coded, grad, master, momentum)
    quarters = exchange(copies(quarter, 4), "x")
    (new_global,) = call(place_kernel, "place", [((2, 32, D), bf16)], [VMEM], [HBM], [dma((4,))])(quarters)
    return (new_global, new_master, new_momentum)


def solution(mesh):
    split = Mesh(mesh.devices.reshape(4, 4, 4, 4, 2), ("x", "u", "v", "y", "c"))
    replica, fsdp = ("x", "u", "v"), ("y", "c")
    placed = (
        P(replica, None, fsdp, None),
        P(replica, None, fsdp, None),
        P(),
        P(None, fsdp, replica),
        P(None, fsdp, replica),
    )
    return jax.shard_map(
        shards,
        mesh=split,
        in_specs=placed,
        out_specs=(P(None, fsdp, None), P(None, fsdp, replica), P(None, fsdp, replica)),
        check_vma=False,
    )
```

time: 123 us -> 113 us (0.919); the launches traced: 121 us -> 112 us
  blocking collectives: 113 us -> 106 us
  local copies, waits for them, and re-layouts: 3.45 us -> 0.13 us
  Pallas kernels: 3.77 us -> 5.14 us
    all_to_all x6 -> x4, blocking collectives: 113 us -> 67.2 us  [exchange(): return lax.all_to_all(blocks, axes, 0, 0, tiled=True)]
    all_gather x0 -> x2, blocking collectives: none -> 39.2 us  [the longest x1 25.7 us: shards(): far = lax.all_gather(packed, 'u', axis=0)]
    unnamed x10 -> x6, local copies, waits for them, and re-layouts: 3.11 us -> 0.02 us
    pallas_call x6 -> x7, Pallas kernels: 3.77 us -> 5.14 us  [the longest x1 2.68 us: shards(): call(term_kernel, 'term', [((4, 2, 32, 2048), bf16), ((8, 128), f32)], [S...]
where the time goes in v3:
time: 113 us; the launch traced here: 112 us
  blocking collectives  106 us (94%)
  Pallas kernels  5.14 us (5%)
    all_to_all x4, blocking collectives, exchange(): return lax.all_to_all(blocks, axes, 0, 0, tiled=True)  67.2 us
    all_gather x1, blocking collectives, shards(): far = lax.all_gather(packed, 'u', axis=0)  25.7 us
    all_gather x1, blocking collectives, shards(): coded = lax.all_gather(coded, 'v', axis=0)  13.5 us
    pallas_call x1, Pallas kernels, shards(): call(term_kernel, 'term', [((4, 2, 32, 2048), bf16), ((8, 128), f32)], [S...  2.68 us

profile of v3, /device:TPU:1, one launch (start us, length us, event | category | flops | bytes accessed | tf_op | source)
XLA Modules:
  0.0 112.4 jit_solution(10828778504631481130)
XLA Ops:
  0.6 2.7 %term.1 = (bf16[4,2,32,2048]{3,2,1,0:T(8,128)(2,1)}, f32[8,128]{1,0:T(8,128)}) custom-call(s32[1]{0:T(128)} %bitcast.1.position_ref, s32[1,64]{1,0:T(1,128)} %bitcast.8, bf16[1,2,32,8192]{3,2,1,0:T(8,128)(2,1)} %anchor_ref.1, bf16[1,2,32,8192]{3,2,1,0:T(8,128)(2,1)} %local_ref.1), custom_call_target="tpu_custom_call" | custom-call | tf_op jit(solution)/shard_map/term/pallas_call | solution.py:177
  3.3 14.6 %all_to_all.20.near_ref = bf16[4,2,32,2048]{3,2,1,0:T(8,128)(2,1)S(1)} all-to-all(bf16[4,2,32,2048]{3,2,1,0:T(8,128)(2,1)} %get-tuple-element.11), channel_id=1, replica_groups=mesh['x'=4,'u'=4,'v'=4,'y'=4,'c'=2] {'x'}, dimensions={0} | all-to-all | bytes 2097152 | tf_op jit(solution)/shard_map/all_to_all | solution.py:17
  17.9 0.3 near.1
  18.2 0.0 copy-start
  18.2 0.0 copy-start.1
  18.2 16.5 %all_to_all.21.coded_ref = s16[4,272,128]{2,1,0:T(8,128)(2,1)S(1)} all-to-all(s16[4,272,128]{2,1,0:T(8,128)(2,1)S(1)} %near.1), channel_id=1, replica_groups=mesh['x'=4,'u'=4,'v'=4,'y'=4,'c'=2] {'v'}, dimensions={0} | all-to-all | bytes 557056 | tf_op jit(solution)/shard_map/all_to_all | solution.py:17
  34.7 0.0 copy-done
  34.7 0.0 copy-done.1
  34.7 0.2 far.1
  34.9 0.0 copy-start.2
  34.9 25.7 %all-gather = s16[1344,128]{1,0:T(8,128)(2,1)S(1)} all-gather(s16[336,128]{1,0:T(8,128)(2,1)S(1)} %far.1), channel_id=2, replica_groups=mesh['x'=4,'u'=4,'v'=4,'y'=4,'c'=2] {'u'}, dimensions={0}, use_global_device_ids=true | all-gather | bytes 430080 | tf_op jit(solution)/shard_map/all_gather | solution.py:190
  60.6 0.0 copy-done.2
  60.6 0.1 grad.1
  60.7 13.5 %all-gather.1 = s16[2112,128]{1,0:T(8,128)(2,1)S(1)} all-gather(s16[528,128]{1,0:T(8,128)(2,1)S(1)} %get-tuple-element.12), channel_id=3, replica_groups=mesh['x'=4,'u'=4,'v'=4,'y'=4,'c'=2] {'v'}, dimensions={0}, use_global_device_ids=true | all-gather | bytes 675840 | tf_op jit(solution)/shard_map/all_gather | solution.py:194
  74.3 0.2 squares.1
  74.5 19.5 %all_to_all.22.parts_ref = f32[32,1,128]{2,1,0:T(1,128)S(1)} all-to-all(f32[32,1,128]{2,1,0:T(1,128)S(1)} %squares.1), channel_id=1, replica_groups=mesh['x'=4,'u'=4,'v'=4,'y'=4,'c'=2] {'x','y','c'}, dimensions={0} | all-to-all | bytes 32768 | tf_op jit(solution)/shard_map/all_to_all | solution.py:17
  93.9 0.7 update.1
  94.6 0.1 broadcast_in_dim.2
  94.8 16.7 %all_to_all.23.quarters_ref = bf16[4,2,32,2048]{3,2,1,0:T(8,128)(2,1)S(1)} all-to-all(bf16[4,2,32,2048]{3,2,1,0:T(8,128)(2,1)S(1)} %broadcast_in_dim.2), channel_id=1, replica_groups=mesh['x'=4,'u'=4,'v'=4,'y'=4,'c'=2] {'x'}, dimensions={0} | all-to-all | bytes 2097152 | tf_op jit(solution)/shard_map/all_to_all | solution.py:17
  111.4 1.0 place.1
Async XLA Ops:
  18.2 16.5 %copy-start = (f32[2,32,128]{2,1,0:T(8,128)S(1)}, f32[2,32,128]{2,1,0:T(8,128)}, u32[]{:S(2)}) copy-start(f32[2,32,128]{2,1,0:T(8,128)} %master_ref.3) | copy-start | bytes 98308
  18.2 16.5 %copy-start.1 = (f32[2,32,128]{2,1,0:T(8,128)S(1)}, f32[2,32,128]{2,1,0:T(8,128)}, u32[]{:S(2)}) copy-start(f32[2,32,128]{2,1,0:T(8,128)} %momentum_ref.3) | copy-start | bytes 98308
  34.9 25.7 %copy-start.2 = (f32[8,128]{1,0:T(8,128)S(1)}, f32[8,128]{1,0:T(8,128)}, u32[]{:S(2)}) copy-start(f32[8,128]{1,0:T(8,128)} %get-tuple-element.10.total_ref) | copy-start | bytes 12292

commit v4 on v3

v4 whole, which is shorter than its diff:
```python
import jax
import jax.numpy as jnp
from jax import lax
from jax.experimental import pallas as pl
from jax.experimental.pallas import tpu as pltpu
from jax.sharding import Mesh, PartitionSpec as P

D = 8192
ROWS = 256
LEVELS = 32000.0
VMEM = pl.BlockSpec(memory_space=pltpu.VMEM)
SMEM = pl.BlockSpec(memory_space=pltpu.SMEM)
HBM = pl.BlockSpec(memory_space=pltpu.HBM)


def exchange(blocks, axes):
    return lax.all_to_all(blocks, axes, 0, 0, tiled=True)


def copies(block, count):
    return jnp.broadcast_to(block[None], (count,) + block.shape)


def encode(values):
    largest = jnp.max(jnp.abs(values), axis=0, keepdims=True)
    exponent = jnp.clip(jnp.floor(jnp.log2(largest) + 0.002) + 1.0, -126.0, 128.0)
    half = jnp.exp2(-0.5 * exponent)
    coded = jnp.round(values * half * half * LEVELS)
    return coded.astype(jnp.int32).astype(jnp.int16), exponent


def pack_exponents(exponents):
    rows = exponents + [jnp.zeros((16 - len(exponents), 128), jnp.float32)]
    return jnp.concatenate(rows, axis=0).astype(jnp.int32).astype(jnp.int16)


def widen(coded):
    return coded.astype(jnp.int32).astype(jnp.float32)


def decode(coded, exponent):
    half = jnp.exp2(0.5 * exponent)
    return widen(coded) * (half * (1.0 / LEVELS)) * half


def decode_sum(ref, senders, block):
    result = None
    for sender in range(senders):
        exponent = widen(ref[sender, 256:272, :])[block : block + 1]
        part = decode(ref[sender, 64 * block : 64 * block + 64, :], exponent)
        result = part if result is None else result + part
    return result


def term_kernel(position_ref, staleness_ref, anchor_ref, local_ref, term_ref, total_ref, stale, anchors, locals_, sems, stale_sem):
    first = pltpu.make_async_copy(staleness_ref, stale, stale_sem)
    first.start()
    pending = []
    for quarter in range(4):
        columns = pl.ds(2048 * quarter, 2048)
        pair = (
            pltpu.make_async_copy(anchor_ref.at[0, :, :, columns], anchors.at[quarter], sems.at[0, quarter]),
            pltpu.make_async_copy(local_ref.at[0, :, :, columns], locals_.at[quarter], sems.at[1, quarter]),
        )
        pair[0].start()
        pair[1].start()
        pending.append(pair)
    first.wait()
    weights = 1.0 / jnp.sqrt(1.0 + stale[...].astype(jnp.float32))
    lane = lax.broadcasted_iota(jnp.int32, (1, 64), 1)
    own = jnp.sum(jnp.where(lane == position_ref[0], weights, 0.0), axis=1, keepdims=True)
    total_ref[...] = jnp.broadcast_to(jnp.sum(weights, axis=1, keepdims=True), (8, 128))
    for quarter in range(4):
        pending[quarter][0].wait()
        pending[quarter][1].wait()
        for half in range(2):
            delta = anchors[quarter, half].astype(jnp.float32) - locals_[quarter, half].astype(jnp.float32)
            term = (own * delta).astype(jnp.bfloat16)
            for z in range(16):
                term_ref[2 * quarter + z % 2, z // 2, half] = term[:, 128 * z : 128 * z + 128]


def near_kernel(near_ref, coded_ref):
    for m in range(2):
        exponents = []
        for u in range(4):
            total = near_ref[0, 2 * u + m].astype(jnp.float32)
            for sender in range(1, 8):
                total = total + near_ref[sender, 2 * u + m].astype(jnp.float32)
            coded_ref[m, 64 * u : 64 * u + 64, :], exponent = encode(total.reshape(64, 128))
            exponents.append(exponent)
        coded_ref[m, 256:272, :] = pack_exponents(exponents)


def far_kernel(coded_ref, master_ref, momentum_ref, out_ref):
    exponents = []
    for u in range(4):
        out_ref[64 * u : 64 * u + 64, :], exponent = encode(decode_sum(coded_ref, 2, u))
        exponents.append(exponent)
    base = master_ref[...] - (0.7 * 0.9 * 0.9) * momentum_ref[...]
    out_ref[272:336, :], exponent = encode(base.reshape(64, 128))
    out_ref[256:272, :] = pack_exponents(exponents + [exponent])


def grad_kernel(total_ref, far_ref, grad_ref, squares_ref):
    squares = jnp.zeros((64, 128), jnp.float32)
    for u in range(4):
        grad = decode_sum(far_ref, 4, u) / total_ref[0:1, :]
        grad_ref[u] = grad
        squares = squares + grad * grad
    squares = jnp.sum(jnp.sum(squares, axis=0, keepdims=True), axis=1, keepdims=True)
    squares_ref[...] = jnp.broadcast_to(squares[None], (128, 1, 128))


def update_kernel(mine_ref, parts_ref, far_ref, grad_ref, master_ref, momentum_ref, blocks_ref, new_master_ref, new_momentum_ref):
    norm = jnp.sqrt(jnp.sum(parts_ref[...], axis=0))
    limit = 0.001 * float(2 * ROWS * D) ** 0.5
    factor = jnp.minimum(1.0, limit / (norm + 1e-06))
    for u in range(4):
        base = decode(far_ref[u, 272:336, :], widen(far_ref[u, 256:272, :])[4:5])
        blocks_ref[u] = (base - (0.7 * 1.9) * (grad_ref[u] * factor)).astype(jnp.bfloat16)
    clipped = (grad_ref[mine_ref[0]] * factor).reshape(2, 32, 128)
    new_momentum = 0.9 * momentum_ref[...] + clipped
    new_momentum_ref[...] = new_momentum
    new_master_ref[...] = master_ref[...] - 0.7 * (clipped + 0.9 * new_momentum)


def place_kernel(blocks_ref, out_ref, quarters, sems):
    pending = []
    for x in range(4):
        for z in range(16):
            block = blocks_ref[2 * x + z % 2, (z // 2) % 2, z // 4]
            quarters[x, :, :, 128 * z : 128 * z + 128] = block.reshape(2, 32, 128)
        copy = pltpu.make_async_copy(quarters.at[x], out_ref.at[:, :, pl.ds(2048 * x, 2048)], sems.at[x])
        copy.start()
        pending.append(copy)
    for copy in pending:
        copy.wait()


def call(kernel, name, outs, in_specs, out_specs, scratch=(), mib=6):
    return pl.pallas_call(
        kernel,
        out_shape=[jax.ShapeDtypeStruct(shape, dtype) for shape, dtype in outs],
        in_specs=in_specs,
        out_specs=out_specs,
        scratch_shapes=scratch,
        name=name,
        compiler_params=pltpu.CompilerParams(vmem_limit_bytes=mib * 2**20),
    )


def shards(anchor, local_params, staleness, master, momentum):
    position = lax.axis_index(("x", "u", "m", "p")).astype(jnp.int32).reshape(1)
    mine = lax.axis_index("u").astype(jnp.int32).reshape(1)
    f32, bf16, i16 = jnp.float32, jnp.bfloat16, jnp.int16
    held = pltpu.VMEM((4, 2, 32, 2048), bf16)
    dma = pltpu.SemaphoreType.DMA
    term, total = call(
        term_kernel,
        "term",
        [((8, 8, 2, 32, 128), bf16), ((8, 128), f32)],
        [SMEM, HBM, HBM, HBM],
        [VMEM, VMEM],
        [pltpu.VMEM((1, 64), jnp.int32), held, held, dma((2, 4)), dma(())],
        mib=56,
    )(position, staleness.reshape(1, 64), anchor, local_params)
    near = exchange(term, ("x", "p"))
    (coded,) = call(near_kernel, "near", [((2, 272, 128), i16)], [VMEM], [VMEM])(near)
    coded = exchange(coded, "m")
    (packed,) = call(far_kernel, "far", [((336, 128), i16)], [VMEM] * 3, [VMEM])(coded, master, momentum)
    far = lax.all_gather(packed, "u", axis=0)
    grad, squares = call(
        grad_kernel, "grad", [((4, 64, 128), f32), ((128, 1, 128), f32)], [VMEM] * 2, [VMEM] * 2
    )(total, far)
    parts = exchange(squares, ("x", "m", "p", "y", "c"))
    blocks, new_master, new_momentum = call(
        update_kernel,
        "update",
        [((4, 64, 128), bf16), ((2, 32, 128), f32), ((2, 32, 128), f32)],
        [SMEM] + [VMEM] * 5,
        [VMEM] * 3,
    )(mine, parts, far, grad, master, momentum)
    blocks = lax.all_gather(blocks, "m", axis=0)
    blocks = exchange(copies(blocks, 8), ("x", "p"))
    (new_global,) = call(place_kernel, "place", [((2, 32, D), bf16)], [VMEM], [HBM], [held, dma((4,))])(blocks.reshape(8, 2, 4, 64, 128))
    return (new_global, new_master, new_momentum)


def solution(mesh):
    split = Mesh(mesh.devices.reshape(4, 4, 2, 2, 4, 2), ("x", "u", "m", "p", "y", "c"))
    replica, fsdp = ("x", "u", "m", "p"), ("y", "c")
    placed = (
        P(replica, None, fsdp, None),
        P(replica, None, fsdp, None),
        P(),
        P(None, fsdp, replica),
        P(None, fsdp, replica),
    )
    return jax.shard_map(
        shards,
        mesh=split,
        in_specs=placed,
        out_specs=(P(None, fsdp, None), P(None, fsdp, replica), P(None, fsdp, replica)),
        check_vma=False,
    )
```

time: 113 us -> 108 us (0.956)
  blocking collectives: 106 us -> 101 us
    all_gather x1, blocking collectives: 13.5 us -> 6.48 us  [shards(): blocks = lax.all_gather(blocks, 'm', axis=0)]
    all_to_all x4, blocking collectives: 67.2 us -> 70.4 us  [exchange(): return lax.all_to_all(blocks, axes, 0, 0, tiled=True)]
    all_gather x1, blocking collectives: 25.7 us -> 24.2 us  [shards(): far = lax.all_gather(packed, 'u', axis=0)]
    pallas_call x6 -> x5, Pallas kernels: 4.99 us -> 4.95 us  [the longest x1 2.68 us: shards(): call(term_kernel, 'term', [((8, 8, 2, 32, 128), bf16), ((8, 128), f32)],...]
where the time goes in v4:
time: 108 us; the launch traced here: 107 us
  blocking collectives  101 us (94%)
  Pallas kernels  5.06 us (5%)
    all_to_all x4, blocking collectives, exchange(): return lax.all_to_all(blocks, axes, 0, 0, tiled=True)  70.4 us
    all_gather x1, blocking collectives, shards(): far = lax.all_gather(packed, 'u', axis=0)  24.2 us
    all_gather x1, blocking collectives, shards(): blocks = lax.all_gather(blocks, 'm', axis=0)  6.48 us
    pallas_call x1, Pallas kernels, shards(): call(term_kernel, 'term', [((8, 8, 2, 32, 128), bf16), ((8, 128), f32)],...  2.68 us

profile of v4, /device:TPU:1, one launch (start us, length us, event | category | flops | bytes accessed | tf_op | source)
XLA Modules:
  0.0 107.2 jit_solution(3330252726248072208)
XLA Ops:
  0.6 2.7 %term.1 = (bf16[8,8,2,32,128]{4,3,2,1,0:T(8,128)(2,1)}, f32[8,128]{1,0:T(8,128)}) custom-call(s32[1]{0:T(128)} %bitcast.1.position_ref, s32[1,64]{1,0:T(1,128)} %bitcast.8, bf16[1,2,32,8192]{3,2,1,0:T(8,128)(2,1)} %anchor_ref.1, bf16[1,2,32,8192]{3,2,1,0:T(8,128)(2,1)} %local_ref.1), custom_call_target="tpu_custom_call" | custom-call | tf_op jit(solution)/shard_map/term/pallas_call | solution.py:159
  3.3 17.8 %all_to_all.20.near_ref = bf16[8,8,2,32,128]{4,3,2,1,0:T(8,128)(2,1)S(1)} all-to-all(bf16[8,8,2,32,128]{4,3,2,1,0:T(8,128)(2,1)} %get-tuple-element.11), channel_id=1, replica_groups=mesh['x'=4,'u'=4,'m'=2,'p'=2,'y'=4,'c'=2] {'x','p'}, dimensions={0} | all-to-all | bytes 2097152 | tf_op jit(solution)/shard_map/all_to_all | solution.py:17
  21.1 0.2 near.1
  21.3 0.0 copy-start
  21.4 0.0 copy-start.1
  21.4 12.4 %all_to_all.21.coded_ref = s16[2,272,128]{2,1,0:T(8,128)(2,1)S(1)} all-to-all(s16[2,272,128]{2,1,0:T(8,128)(2,1)S(1)} %near.1), channel_id=1, replica_groups=mesh['x'=4,'u'=4,'m'=2,'p'=2,'y'=4,'c'=2] {'m'}, dimensions={0} | all-to-all | bytes 278528 | tf_op jit(solution)/shard_map/all_to_all | solution.py:17
  33.8 0.0 copy-done
  33.8 0.0 copy-done.1
  33.8 0.1 far.1
  33.9 0.0 copy-start.2
  33.9 24.2 %all-gather = s16[1344,128]{1,0:T(8,128)(2,1)S(1)} all-gather(s16[336,128]{1,0:T(8,128)(2,1)S(1)} %far.1), channel_id=2, replica_groups=mesh['x'=4,'u'=4,'m'=2,'p'=2,'y'=4,'c'=2] {'u'}, dimensions={0}, use_global_device_ids=true | all-gather | bytes 430080 | tf_op jit(solution)/shard_map/all_gather | solution.py:172
  58.1 0.0 copy-done.2
  58.1 0.2 grad.1
  58.4 23.0 %all_to_all.22.parts_ref = f32[128,1,128]{2,1,0:T(1,128)S(1)} all-to-all(f32[128,1,128]{2,1,0:T(1,128)S(1)} %get-tuple-element.12), channel_id=1, replica_groups=mesh['x'=4,'u'=4,'m'=2,'p'=2,'y'=4,'c'=2] {'x','m','p','y','c'}, dimensions={0} | all-to-all | bytes 131072 | tf_op jit(solution)/shard_map/all_to_all | solution.py:17
  81.3 0.8 update.1
  82.1 6.5 %all-gather.1 = bf16[8,64,128]{2,1,0:T(8,128)(2,1)S(1)} all-gather(bf16[4,64,128]{2,1,0:T(8,128)(2,1)S(1)} %get-tuple-element.14), channel_id=3, replica_groups=mesh['x'=4,'u'=4,'m'=2,'p'=2,'y'=4,'c'=2] {'m'}, dimensions={0}, use_global_device_ids=true | all-gather | bytes 196608 | tf_op jit(solution)/shard_map/all_gather | solution.py:184
  88.6 0.2 broadcast_in_dim.2
  88.8 17.3 %all_to_all.23.blocks_ref = bf16[8,2,4,64,128]{4,3,2,1,0:T(8,128)(2,1)S(1)} all-to-all(bf16[8,2,4,64,128]{4,3,2,1,0:T(8,128)(2,1)S(1)} %broadcast_in_dim.2), channel_id=1, replica_groups=mesh['x'=4,'u'=4,'m'=2,'p'=2,'y'=4,'c'=2] {'x','p'}, dimensions={0} | all-to-all | bytes 2097152 | tf_op jit(solution)/shard_map/all_to_all | solution.py:17
  106.1 1.0 place.1
Async XLA Ops:
  21.3 12.4 %copy-start = (f32[2,32,128]{2,1,0:T(8,128)S(1)}, f32[2,32,128]{2,1,0:T(8,128)}, u32[]{:S(2)}) copy-start(f32[2,32,128]{2,1,0:T(8,128)} %master_ref.3) | copy-start | bytes 98308
  21.4 12.4 %copy-start.1 = (f32[2,32,128]{2,1,0:T(8,128)S(1)}, f32[2,32,128]{2,1,0:T(8,128)}, u32[]{:S(2)}) copy-start(f32[2,32,128]{2,1,0:T(8,128)} %momentum_ref.3) | copy-start | bytes 98308
  33.9 24.2 %copy-start.2 = (f32[8,128]{1,0:T(8,128)S(1)}, f32[8,128]{1,0:T(8,128)}, u32[]{:S(2)}) copy-start(f32[8,128]{1,0:T(8,128)} %get-tuple-element.10.total_ref) | copy-start | bytes 12292

commit v5 on v4

--- a/solution.py
+++ b/solution.py
@@ -102,23 +102,32 @@
     out_ref[256:272, :] = pack_exponents(exponents + [exponent])
 
 
-def grad_kernel(total_ref, far_ref, grad_ref, squares_ref):
+def grad_kernel(total_ref, far_ref, grad_ref, coded_ref, squares_ref):
     squares = jnp.zeros((64, 128), jnp.float32)
+    exponents, base_exponents = [], []
     for u in range(4):
         grad = decode_sum(far_ref, 4, u) / total_ref[0:1, :]
         grad_ref[u] = grad
         squares = squares + grad * grad
+        coded_ref[64 * u : 64 * u + 64, :], exponent = encode(grad)
+        exponents.append(exponent)
+        coded_ref[272 + 64 * u : 336 + 64 * u, :] = far_ref[u, 272:336, :]
+        base_exponents.append(widen(far_ref[u, 256:272, :])[4:5])
+    coded_ref[256:272, :] = pack_exponents(exponents + base_exponents)
     squares = jnp.sum(jnp.sum(squares, axis=0, keepdims=True), axis=1, keepdims=True)
     squares_ref[...] = jnp.broadcast_to(squares[None], (128, 1, 128))
 
 
-def update_kernel(mine_ref, parts_ref, far_ref, grad_ref, master_ref, momentum_ref, blocks_ref, new_master_ref, new_momentum_ref):
+def update_kernel(mine_ref, parts_ref, coded_ref, grad_ref, master_ref, momentum_ref, blocks_ref, new_master_ref, new_momentum_ref):
     norm = jnp.sqrt(jnp.sum(parts_ref[...], axis=0))
     limit = 0.001 * float(2 * ROWS * D) ** 0.5
     factor = jnp.minimum(1.0, limit / (norm + 1e-06))
-    for u in range(4):
-        base = decode(far_ref[u, 272:336, :], widen(far_ref[u, 256:272, :])[4:5])
-        blocks_ref[u] = (base - (0.7 * 1.9) * (grad_ref[u] * factor)).astype(jnp.bfloat16)
+    for m in range(2):
+        exponents = widen(coded_ref[m, 256:272, :])
+        for u in range(4):
+            base = decode(coded_ref[m, 272 + 64 * u : 336 + 64 * u, :], exponents[4 + u : 5 + u])
+            grad = decode(coded_ref[m, 64 * u : 64 * u + 64, :], exponents[u : u + 1])
+            blocks_ref[m, u] = (base - (0.7 * 1.9) * (grad * factor)).astype(jnp.bfloat16)
     clipped = (grad_ref[mine_ref[0]] * factor).reshape(2, 32, 128)
     new_momentum = 0.9 * momentum_ref[...] + clipped
     new_momentum_ref[...] = new_momentum
@@ -170,18 +179,22 @@
     coded = exchange(coded, "m")
     (packed,) = call(far_kernel, "far", [((336, 128), i16)], [VMEM] * 3, [VMEM])(coded, master, momentum)
     far = lax.all_gather(packed, "u", axis=0)
-    grad, squares = call(
-        grad_kernel, "grad", [((4, 64, 128), f32), ((128, 1, 128), f32)], [VMEM] * 2, [VMEM] * 2
+    grad, coded, squares = call(
+        grad_kernel,
+        "grad",
+        [((4, 64, 128), f32), ((528, 128), i16), ((128, 1, 128), f32)],
+        [VMEM] * 2,
+        [VMEM] * 3,
     )(total, far)
     parts = exchange(squares, ("x", "m", "p", "y", "c"))
+    coded = lax.all_gather(coded, "m", axis=0)
     blocks, new_master, new_momentum = call(
         update_kernel,
         "update",
-        [((4, 64, 128), bf16), ((2, 32, 128), f32), ((2, 32, 128), f32)],
+        [((2, 4, 64, 128), bf16), ((2, 32, 128), f32), ((2, 32, 128), f32)],
         [SMEM] + [VMEM] * 5,
         [VMEM] * 3,
-    )(mine, parts, far, grad, master, momentum)
-    blocks = lax.all_gather(blocks, "m", axis=0)
+    )(mine, parts, coded, grad, master, momentum)
     blocks = exchange(copies(blocks, 8), ("x", "p"))
     (new_global,) = call(place_kernel, "place", [((2, 32, D), bf16)], [VMEM], [HBM], [held, dma((4,))])(blocks.reshape(8, 2, 4, 64, 128))
     return (new_global, new_master, new_momentum)

time: 108 us -> 105 us (0.972)
  blocking collectives: 101 us -> 83.6 us
  starting transfers between devices: 0 us -> 13.4 us
    all_to_all x4 -> x3, blocking collectives: 70.4 us -> 49.5 us  [exchange(): return lax.all_to_all(blocks, axes, 0, 0, tiled=True)]
    all_to_all x0 -> x1, starting transfers between devices: none -> 13.4 us  [exchange(): return lax.all_to_all(blocks, axes, 0, 0, tiled=True)]
    all_gather x1, blocking collectives: 6.48 us -> 9.86 us  [shards(): coded = lax.all_gather(coded, 'm', axis=0)]
  transfers between devices with their start and end apart: 0 -> 1, of which waited for: 0 -> 0; matrix products, arithmetic and copies ran while one was open for 0% -> 0% of each run, Pallas kernels for 0% -> 0%
where the time goes in v5:
time: 105 us; the launch traced here: 104 us
  blocking collectives  83.6 us (80%)
  starting transfers between devices  13.4 us (13%)
  Pallas kernels  5.69 us (5%)
    all_to_all x3, blocking collectives, exchange(): return lax.all_to_all(blocks, axes, 0, 0, tiled=True)  49.5 us
    all_gather x1, blocking collectives, shards(): far = lax.all_gather(packed, 'u', axis=0)  24.2 us
    all_to_all x1, starting transfers between devices, exchange(): return lax.all_to_all(blocks, axes, 0, 0, tiled=True)  13.4 us
    all_gather x1, blocking collectives, shards(): coded = lax.all_gather(coded, 'm', axis=0)  9.86 us
    pallas_call x1, Pallas kernels, shards(): call(term_kernel, 'term', [((8, 8, 2, 32, 128), bf16), ((8, 128), f32)],...  2.68 us
  transfers between devices with their start and end apart: 1, of which 0 were waited for; matrix products, arithmetic and copies ran while one was open for 0% of the time, Pallas kernels for 0%

profile of v5, /device:TPU:1, one launch (start us, length us, event | category | flops | bytes accessed | tf_op | source)
XLA Modules:
  0.0 103.7 jit_solution(6374730180338425552)
XLA Ops:
  0.6 2.7 %term.1 = (bf16[8,8,2,32,128]{4,3,2,1,0:T(8,128)(2,1)}, f32[8,128]{1,0:T(8,128)}) custom-call(s32[1]{0:T(128)} %bitcast.1.position_ref, s32[1,64]{1,0:T(1,128)} %bitcast.7, bf16[1,2,32,8192]{3,2,1,0:T(8,128)(2,1)} %anchor_ref.1, bf16[1,2,32,8192]{3,2,1,0:T(8,128)(2,1)} %local_ref.1), custom_call_target="tpu_custom_call" | custom-call | tf_op jit(solution)/shard_map/term/pallas_call | solution.py:168
  3.3 17.8 %all_to_all.20.near_ref = bf16[8,8,2,32,128]{4,3,2,1,0:T(8,128)(2,1)S(1)} all-to-all(bf16[8,8,2,32,128]{4,3,2,1,0:T(8,128)(2,1)} %get-tuple-element.12), channel_id=1, replica_groups=mesh['x'=4,'u'=4,'m'=2,'p'=2,'y'=4,'c'=2] {'x','p'}, dimensions={0} | all-to-all | bytes 2097152 | tf_op jit(solution)/shard_map/all_to_all | solution.py:17
  21.1 0.2 near.1
  21.3 0.0 copy-start
  21.4 0.0 copy-start.1
  21.4 12.4 %all_to_all.21.coded_ref = s16[2,272,128]{2,1,0:T(8,128)(2,1)S(1)} all-to-all(s16[2,272,128]{2,1,0:T(8,128)(2,1)S(1)} %near.1), channel_id=1, replica_groups=mesh['x'=4,'u'=4,'m'=2,'p'=2,'y'=4,'c'=2] {'m'}, dimensions={0} | all-to-all | bytes 278528 | tf_op jit(solution)/shard_map/all_to_all | solution.py:17
  33.8 0.0 copy-done
  33.8 0.0 copy-done.1
  33.8 0.1 far.1
  33.9 0.0 copy-start.2
  33.9 24.2 %all-gather = s16[1344,128]{1,0:T(8,128)(2,1)S(1)} all-gather(s16[336,128]{1,0:T(8,128)(2,1)S(1)} %far.1), channel_id=2, replica_groups=mesh['x'=4,'u'=4,'m'=2,'p'=2,'y'=4,'c'=2] {'u'}, dimensions={0}, use_global_device_ids=true | all-gather | bytes 430080 | tf_op jit(solution)/shard_map/all_gather | solution.py:181
  58.1 0.0 copy-done.2
  58.1 0.9 grad.1
  59.0 13.4 %all-to-all-start.2 = ((f32[128,1,128]{2,1,0:T(1,128)}), f32[128,1,128]{2,1,0:T(1,128)S(1)}, u32[]{:S(2)}, u32[]{:S(2)}) async-start(f32[128,1,128]{2,1,0:T(1,128)} %get-tuple-element.13), calls=%async_computation.2 | async-start | bytes 131072 | tf_op jit(solution)/shard_map/all_to_all | solution.py:17
  72.4 9.9 %all-gather.1 = s16[1056,128]{1,0:T(8,128)(2,1)S(1)} all-gather(s16[528,128]{1,0:T(8,128)(2,1)S(1)} %get-tuple-element.14), channel_id=3, replica_groups=mesh['x'=4,'u'=4,'m'=2,'p'=2,'y'=4,'c'=2] {'m'}, dimensions={0}, use_global_device_ids=true | all-gather | bytes 405504 | tf_op jit(solution)/shard_map/all_gather | solution.py:190
  82.2 0.0 all-to-all-done.2.parts_ref
  82.2 0.8 update.1
  83.0 0.2 broadcast_in_dim.2
  83.3 19.3 %all_to_all.22.blocks_ref = bf16[8,2,4,64,128]{4,3,2,1,0:T(8,128)(2,1)S(1)} all-to-all(bf16[8,2,4,64,128]{4,3,2,1,0:T(8,128)(2,1)S(1)} %broadcast_in_dim.2), channel_id=1, replica_groups=mesh['x'=4,'u'=4,'m'=2,'p'=2,'y'=4,'c'=2] {'x','p'}, dimensions={0} | all-to-all | bytes 2097152 | tf_op jit(solution)/shard_map/all_to_all | solution.py:17
  102.6 1.0 %place.1 = bf16[2,32,8192]{2,1,0:T(8,128)(2,1)} custom-call(bf16[8,2,4,64,128]{4,3,2,1,0:T(8,128)(2,1)S(1)} %all_to_all.22.blocks_ref), custom_call_target="tpu_custom_call" | custom-call | tf_op jit(solution)/shard_map/place/pallas_call | solution.py:199
Async XLA Ops:
  21.3 12.4 %copy-start = (f32[2,32,128]{2,1,0:T(8,128)S(1)}, f32[2,32,128]{2,1,0:T(8,128)}, u32[]{:S(2)}) copy-start(f32[2,32,128]{2,1,0:T(8,128)} %master_ref.3) | copy-start | bytes 98308
  21.4 12.4 %copy-start.1 = (f32[2,32,128]{2,1,0:T(8,128)S(1)}, f32[2,32,128]{2,1,0:T(8,128)}, u32[]{:S(2)}) copy-start(f32[2,32,128]{2,1,0:T(8,128)} %momentum_ref.3) | copy-start | bytes 98308
  33.9 24.2 %copy-start.2 = (f32[8,128]{1,0:T(8,128)S(1)}, f32[8,128]{1,0:T(8,128)}, u32[]{:S(2)}) copy-start(f32[8,128]{1,0:T(8,128)} %get-tuple-element.11.total_ref) | copy-start | bytes 12292
  59.0 23.2 %all-to-all-start.2 = ((f32[128,1,128]{2,1,0:T(1,128)}), f32[128,1,128]{2,1,0:T(1,128)S(1)}, u32[]{:S(2)}, u32[]{:S(2)}) async-start(f32[128,1,128]{2,1,0:T(1,128)} %get-tuple-element.13), calls=%async_computation.2 | async-start | bytes 131072 | tf_op jit(solution)/shard_map/all_to_all | solution.py:17

commit v6 on v5

--- a/solution.py
+++ b/solution.py
@@ -80,7 +80,7 @@
                 term_ref[2 * quarter + z % 2, z // 2, half] = term[:, 128 * z : 128 * z + 128]
 
 
-def near_kernel(near_ref, coded_ref):
+def near_kernel(near_ref, bases_ref, coded_ref, packed_ref):
     for m in range(2):
         exponents = []
         for u in range(4):
@@ -90,42 +90,52 @@
             coded_ref[m, 64 * u : 64 * u + 64, :], exponent = encode(total.reshape(64, 128))
             exponents.append(exponent)
         coded_ref[m, 256:272, :] = pack_exponents(exponents)
-
-
-def far_kernel(coded_ref, master_ref, momentum_ref, out_ref):
+    exponents = []
+    for m in range(2):
+        packed_ref[64 * m : 64 * m + 64, :] = bases_ref[m, :64, :]
+        exponents.append(widen(bases_ref[m, 64:80, :])[0:1])
+    packed_ref[128:144, :] = pack_exponents(exponents)
+
+
+def base_kernel(master_ref, momentum_ref, out_ref):
+    base = master_ref[...] - (0.7 * 0.9 * 0.9) * momentum_ref[...]
+    out_ref[:64, :], exponent = encode(base.reshape(64, 128))
+    out_ref[64:80, :] = pack_exponents([exponent])
+
+
+def far_kernel(coded_ref, bases_ref, out_ref):
     exponents = []
     for u in range(4):
         out_ref[64 * u : 64 * u + 64, :], exponent = encode(decode_sum(coded_ref, 2, u))
         exponents.append(exponent)
-    base = master_ref[...] - (0.7 * 0.9 * 0.9) * momentum_ref[...]
-    out_ref[272:336, :], exponent = encode(base.reshape(64, 128))
-    out_ref[256:272, :] = pack_exponents(exponents + [exponent])
+    out_ref[272:400, :] = bases_ref[:128, :]
+    base_exponents = widen(bases_ref[128:144, :])
+    out_ref[256:272, :] = pack_exponents(exponents + [base_exponents[0:1], base_exponents[1:2]])
 
 
 def grad_kernel(total_ref, far_ref, grad_ref, coded_ref, squares_ref):
     squares = jnp.zeros((64, 128), jnp.float32)
-    exponents, base_exponents = [], []
+    exponents = []
     for u in range(4):
         grad = decode_sum(far_ref, 4, u) / total_ref[0:1, :]
         grad_ref[u] = grad
         squares = squares + grad * grad
         coded_ref[64 * u : 64 * u + 64, :], exponent = encode(grad)
         exponents.append(exponent)
-        coded_ref[272 + 64 * u : 336 + 64 * u, :] = far_ref[u, 272:336, :]
-        base_exponents.append(widen(far_ref[u, 256:272, :])[4:5])
-    coded_ref[256:272, :] = pack_exponents(exponents + base_exponents)
+    coded_ref[256:272, :] = pack_exponents(exponents)
     squares = jnp.sum(jnp.sum(squares, axis=0, keepdims=True), axis=1, keepdims=True)
     squares_ref[...] = jnp.broadcast_to(squares[None], (128, 1, 128))
 
 
-def update_kernel(mine_ref, parts_ref, coded_ref, grad_ref, master_ref, momentum_ref, blocks_ref, new_master_ref, new_momentum_ref):
+def update_kernel(mine_ref, parts_ref, far_ref, coded_ref, grad_ref, master_ref, momentum_ref, blocks_ref, new_master_ref, new_momentum_ref):
     norm = jnp.sqrt(jnp.sum(parts_ref[...], axis=0))
     limit = 0.001 * float(2 * ROWS * D) ** 0.5
     factor = jnp.minimum(1.0, limit / (norm + 1e-06))
     for m in range(2):
         exponents = widen(coded_ref[m, 256:272, :])
         for u in range(4):
-            base = decode(coded_ref[m, 272 + 64 * u : 336 + 64 * u, :], exponents[4 + u : 5 + u])
+            base_exponents = widen(far_ref[u, 256:272, :])
+            base = decode(far_ref[u, 272 + 64 * m : 336 + 64 * m, :], base_exponents[4 + m : 5 + m])
             grad = decode(coded_ref[m, 64 * u : 64 * u + 64, :], exponents[u : u + 1])
             blocks_ref[m, u] = (base - (0.7 * 1.9) * (grad * factor)).astype(jnp.bfloat16)
     clipped = (grad_ref[mine_ref[0]] * factor).reshape(2, 32, 128)
@@ -175,14 +185,18 @@
         mib=56,
     )(position, staleness.reshape(1, 64), anchor, local_params)
     near = exchange(term, ("x", "p"))
-    (coded,) = call(near_kernel, "near", [((2, 272, 128), i16)], [VMEM], [VMEM])(near)
+    (base,) = call(base_kernel, "base", [((80, 128), i16)], [VMEM] * 2, [VMEM])(master, momentum)
+    bases = lax.all_gather(base, "m", axis=0)
+    coded, bases = call(
+        near_kernel, "near", [((2, 272, 128), i16), ((144, 128), i16)], [VMEM] * 2, [VMEM] * 2
+    )(near, bases)
     coded = exchange(coded, "m")
-    (packed,) = call(far_kernel, "far", [((336, 128), i16)], [VMEM] * 3, [VMEM])(coded, master, momentum)
+    (packed,) = call(far_kernel, "far", [((400, 128), i16)], [VMEM] * 2, [VMEM])(coded, bases)
     far = lax.all_gather(packed, "u", axis=0)
     grad, coded, squares = call(
         grad_kernel,
         "grad",
-        [((4, 64, 128), f32), ((528, 128), i16), ((128, 1, 128), f32)],
+        [((4, 64, 128), f32), ((272, 128), i16), ((128, 1, 128), f32)],
         [VMEM] * 2,
         [VMEM] * 3,
     )(total, far)
@@ -192,9 +206,9 @@
         update_kernel,
         "update",
         [((2, 4, 64, 128), bf16), ((2, 32, 128), f32), ((2, 32, 128), f32)],
-        [SMEM] + [VMEM] * 5,
+        [SMEM] + [VMEM] * 6,
         [VMEM] * 3,
-    )(mine, parts, coded, grad, master, momentum)
+    )(mine, parts, far, coded, grad, master, momentum)
     blocks = exchange(copies(blocks, 8), ("x", "p"))
     (new_global,) = call(place_kernel, "place", [((2, 32, D), bf16)], [VMEM], [HBM], [held, dma((4,))])(blocks.reshape(8, 2, 4, 64, 128))
     return (new_global, new_master, new_momentum)

time: 105 us -> 103 us (0.981); the launches traced: 104 us -> 103 us
  blocking collectives: 83.6 us -> 69.2 us
  starting transfers between devices: 13.4 us -> 20.3 us
  waiting for transfers between devices: 0.01 us -> 6.83 us
    all_to_all x3 -> x2, blocking collectives: 49.5 us -> 28.7 us  [exchange(): return lax.all_to_all(blocks, axes, 0, 0, tiled=True)]
    all_gather x0 -> x1, blocking collectives: none -> 7.98 us  [shards(): bases = lax.all_gather(base, 'm', axis=0)]
    all_to_all x1 -> x2, starting transfers between devices: 13.4 us -> 20.3 us  [exchange(): return lax.all_to_all(blocks, axes, 0, 0, tiled=True)]
    all_to_all x1 -> x2, waiting for transfers between devices: 0.01 us -> 6.83 us  [exchange(): return lax.all_to_all(blocks, axes, 0, 0, tiled=True)]
    all_gather x1, blocking collectives: 9.86 us -> 7.05 us  [shards(): coded = lax.all_gather(coded, 'm', axis=0)]
    all_gather x1, blocking collectives: 24.2 us -> 25.5 us  [shards(): far = lax.all_gather(packed, 'u', axis=0)]
  transfers between devices with their start and end apart: 1 -> 2, of which waited for: 0 -> 2; matrix products, arithmetic and copies ran while one was open for 0% -> 0% of each run, Pallas kernels for 0% -> 0%
where the time goes in v6:
time: 103 us
  blocking collectives  69.2 us (67%)
  starting transfers between devices  20.3 us (20%)
  waiting for transfers between devices  6.83 us (7%)
  Pallas kernels  5.72 us (6%)
    all_to_all x2, blocking collectives, exchange(): return lax.all_to_all(blocks, axes, 0, 0, tiled=True)  28.7 us
    all_gather x1, blocking collectives, shards(): far = lax.all_gather(packed, 'u', axis=0)  25.5 us
    all_to_all x2, starting transfers between devices, exchange(): return lax.all_to_all(blocks, axes, 0, 0, tiled=True)  20.3 us
    all_gather x1, blocking collectives, shards(): bases = lax.all_gather(base, 'm', axis=0)  7.98 us
    all_gather x1, blocking collectives, shards(): coded = lax.all_gather(coded, 'm', axis=0)  7.05 us
    all_to_all x2, waiting for transfers between devices, exchange(): return lax.all_to_all(blocks, axes, 0, 0, tiled=True)  6.83 us
    pallas_call x1, Pallas kernels, shards(): call(term_kernel, 'term', [((8, 8, 2, 32, 128), bf16), ((8, 128), f32)],...  2.68 us
  transfers between devices with their start and end apart: 2, of which 2 were waited for; matrix products, arithmetic and copies ran while one was open for 0% of the time, Pallas kernels for 0%

profile of v6, /device:TPU:1, one launch (start us, length us, event | category | flops | bytes accessed | tf_op | source)
XLA Modules:
  0.0 103.1 jit_solution(13202611627551899047)
XLA Ops:
  0.6 2.7 %term.1 = (bf16[8,8,2,32,128]{4,3,2,1,0:T(8,128)(2,1)}, f32[8,128]{1,0:T(8,128)}) custom-call(s32[1]{0:T(128)} %bitcast.1.position_ref, s32[1,64]{1,0:T(1,128)} %bitcast.10, bf16[1,2,32,8192]{3,2,1,0:T(8,128)(2,1)} %anchor_ref.1, bf16[1,2,32,8192]{3,2,1,0:T(8,128)(2,1)} %local_ref.1), custom_call_target="tpu_custom_call" | custom-call | tf_op jit(solution)/shard_map/term/pallas_call | solution.py:178
  3.3 0.0 copy-start
  3.3 0.0 copy-start.1
  3.4 6.2 %all-to-all-start = ((bf16[8,8,2,32,128]{4,3,2,1,0:T(8,128)(2,1)}), bf16[8,8,2,32,128]{4,3,2,1,0:T(8,128)(2,1)S(1)}, u32[]{:S(2)}, u32[]{:S(2)}) async-start(bf16[8,8,2,32,128]{4,3,2,1,0:T(8,128)(2,1)} %get-tuple-element.14), calls=%async_computation | async-start | bytes 2097152 | tf_op jit(solution)/shard_map/all_to_all | solution.py:17
  9.6 0.0 copy-done
  9.6 0.0 copy-done.1
  9.6 8.0 %all-gather = s16[160,128]{1,0:T(8,128)(2,1)S(1)} all-gather(s16[80,128]{1,0:T(8,128)(2,1)S(1)} %base.1), channel_id=2, replica_groups=mesh['x'=4,'u'=4,'m'=2,'p'=2,'y'=4,'c'=2] {'m'}, dimensions={0}, use_global_device_ids=true | all-gather | bytes 61440 | tf_op jit(solution)/shard_map/all_gather | solution.py:189
  17.6 4.2 %all-to-all-done.near_ref = bf16[8,8,2,32,128]{4,3,2,1,0:T(8,128)(2,1)S(1)} async-done(((bf16[8,8,2,32,128]{4,3,2,1,0:T(8,128)(2,1)}), bf16[8,8,2,32,128]{4,3,2,1,0:T(8,128)(2,1)S(1)}, u32[]{:S(2)}, u32[]{:S(2)}) %all-to-all-start) | async-done | bytes 1048608 | tf_op jit(solution)/shard_map/all_to_all | solution.py:17
  21.8 0.2 near.1
  22.0 11.4 %all_to_all.20.coded_ref = s16[2,272,128]{2,1,0:T(8,128)(2,1)S(1)} all-to-all(s16[2,272,128]{2,1,0:T(8,128)(2,1)S(1)} %get-tuple-element.15), channel_id=1, replica_groups=mesh['x'=4,'u'=4,'m'=2,'p'=2,'y'=4,'c'=2] {'m'}, dimensions={0} | all-to-all | bytes 278528 | tf_op jit(solution)/shard_map/all_to_all | solution.py:17
  33.4 0.1 far.1
  33.5 0.0 copy-start.2
  33.5 25.5 %all-gather.1 = s16[1600,128]{1,0:T(8,128)(2,1)S(1)} all-gather(s16[400,128]{1,0:T(8,128)(2,1)S(1)} %far.1), channel_id=3, replica_groups=mesh['x'=4,'u'=4,'m'=2,'p'=2,'y'=4,'c'=2] {'u'}, dimensions={0}, use_global_device_ids=true | all-gather | bytes 512000 | tf_op jit(solution)/shard_map/all_gather | solution.py:195
  59.0 0.0 copy-done.2
  59.0 0.9 grad.1
  59.9 14.1 %all-to-all-start.2 = ((f32[128,1,128]{2,1,0:T(1,128)}), f32[128,1,128]{2,1,0:T(1,128)S(1)}, u32[]{:S(2)}, u32[]{:S(2)}) async-start(f32[128,1,128]{2,1,0:T(1,128)} %get-tuple-element.17), calls=%async_computation.2 | async-start | bytes 131072 | tf_op jit(solution)/shard_map/all_to_all | solution.py:17
  74.0 7.1 %all-gather.2 = s16[544,128]{1,0:T(8,128)(2,1)S(1)} all-gather(s16[272,128]{1,0:T(8,128)(2,1)S(1)} %get-tuple-element.18), channel_id=4, replica_groups=mesh['x'=4,'u'=4,'m'=2,'p'=2,'y'=4,'c'=2] {'m'}, dimensions={0}, use_global_device_ids=true | all-gather | bytes 208896 | tf_op jit(solution)/shard_map/all_gather | solution.py:204
  81.1 2.7 %all-to-all-done.2.parts_ref = f32[128,1,128]{2,1,0:T(1,128)S(1)} async-done(((f32[128,1,128]{2,1,0:T(1,128)}), f32[128,1,128]{2,1,0:T(1,128)S(1)}, u32[]{:S(2)}, u32[]{:S(2)}) %all-to-all-start.2) | async-done | bytes 65568 | tf_op jit(solution)/shard_map/all_to_all | solution.py:17
  83.7 0.8 update.1
  84.5 0.2 broadcast_in_dim.2
  84.7 17.3 %all_to_all.21.blocks_ref = bf16[8,2,4,64,128]{4,3,2,1,0:T(8,128)(2,1)S(1)} all-to-all(bf16[8,2,4,64,128]{4,3,2,1,0:T(8,128)(2,1)S(1)} %broadcast_in_dim.2), channel_id=1, replica_groups=mesh['x'=4,'u'=4,'m'=2,'p'=2,'y'=4,'c'=2] {'x','p'}, dimensions={0} | all-to-all | bytes 2097152 | tf_op jit(solution)/shard_map/all_to_all | solution.py:17
  102.0 1.0 %place.1 = bf16[2,32,8192]{2,1,0:T(8,128)(2,1)} custom-call(bf16[8,2,4,64,128]{4,3,2,1,0:T(8,128)(2,1)S(1)} %all_to_all.21.blocks_ref), custom_call_target="tpu_custom_call" | custom-call | tf_op jit(solution)/shard_map/place/pallas_call | solution.py:213
  (1 shorter events, 0.0 us)
Async XLA Ops:
  3.3 6.2 %copy-start = (f32[2,32,128]{2,1,0:T(8,128)S(1)}, f32[2,32,128]{2,1,0:T(8,128)}, u32[]{:S(2)}) copy-start(f32[2,32,128]{2,1,0:T(8,128)} %master_ref.3) | copy-start | bytes 98308
  3.3 6.2 %copy-start.1 = (f32[2,32,128]{2,1,0:T(8,128)S(1)}, f32[2,32,128]{2,1,0:T(8,128)}, u32[]{:S(2)}) copy-start(f32[2,32,128]{2,1,0:T(8,128)} %momentum_ref.3) | copy-start | bytes 98308
  3.4 18.4 %all-to-all-start = ((bf16[8,8,2,32,128]{4,3,2,1,0:T(8,128)(2,1)}), bf16[8,8,2,32,128]{4,3,2,1,0:T(8,128)(2,1)S(1)}, u32[]{:S(2)}, u32[]{:S(2)}) async-start(bf16[8,8,2,32,128]{4,3,2,1,0:T(8,128)(2,1)} %get-tuple-element.14), calls=%async_computation | async-start | bytes 2097152 | tf_op jit(solution)/shard_map/all_to_all | solution.py:17
  33.5 25.5 %copy-start.2 = (f32[8,128]{1,0:T(8,128)S(1)}, f32[8,128]{1,0:T(8,128)}, u32[]{:S(2)}) copy-start(f32[8,128]{1,0:T(8,128)} %get-tuple-element.13.total_ref) | copy-start | bytes 12292
  59.9 23.8 %all-to-all-start.2 = ((f32[128,1,128]{2,1,0:T(1,128)}), f32[128,1,128]{2,1,0:T(1,128)S(1)}, u32[]{:S(2)}, u32[]{:S(2)}) async-start(f32[128,1,128]{2,1,0:T(1,128)} %get-tuple-element.17), calls=%async_computation.2 | async-start | bytes 131072 | tf_op jit(solution)/shard_map/all_to_all | solution.py:17

commit v7 on v6

--- a/solution.py
+++ b/solution.py
@@ -113,24 +113,38 @@
     out_ref[256:272, :] = pack_exponents(exponents + [base_exponents[0:1], base_exponents[1:2]])
 
 
-def grad_kernel(total_ref, far_ref, grad_ref, coded_ref, squares_ref):
+def grad_kernel(total_ref, far_ref, grad_ref, coded_ref, squares_ref, held, sem):
     squares = jnp.zeros((64, 128), jnp.float32)
-    exponents = []
     for u in range(4):
         grad = decode_sum(far_ref, 4, u) / total_ref[0:1, :]
         grad_ref[u] = grad
         squares = squares + grad * grad
-        coded_ref[64 * u : 64 * u + 64, :], exponent = encode(grad)
+    squares = jnp.sum(jnp.sum(squares, axis=0, keepdims=True), axis=1, keepdims=True)
+    held[...] = jnp.broadcast_to(squares[None], (128, 1, 128))
+    copy = pltpu.make_async_copy(held, squares_ref, sem)
+    copy.start()
+    exponents = []
+    for u in range(4):
+        coded_ref[64 * u : 64 * u + 64, :], exponent = encode(grad_ref[u])
         exponents.append(exponent)
     coded_ref[256:272, :] = pack_exponents(exponents)
-    squares = jnp.sum(jnp.sum(squares, axis=0, keepdims=True), axis=1, keepdims=True)
-    squares_ref[...] = jnp.broadcast_to(squares[None], (128, 1, 128))
-
-
-def update_kernel(mine_ref, parts_ref, far_ref, coded_ref, grad_ref, master_ref, momentum_ref, blocks_ref, new_master_ref, new_momentum_ref):
+    copy.wait()
+
+
+def update_kernel(mine_ref, parts_ref, far_ref, coded_ref, grad_ref, master_ref, momentum_ref, blocks_ref, new_master_ref, new_momentum_ref, held, sems):
     norm = jnp.sqrt(jnp.sum(parts_ref[...], axis=0))
     limit = 0.001 * float(2 * ROWS * D) ** 0.5
     factor = jnp.minimum(1.0, limit / (norm + 1e-06))
+    clipped = (grad_ref[mine_ref[0]] * factor).reshape(2, 32, 128)
+    new_momentum = 0.9 * momentum_ref[...] + clipped
+    held[0] = new_momentum
+    held[1] = master_ref[...] - 0.7 * (clipped + 0.9 * new_momentum)
+    pending = [
+        pltpu.make_async_copy(held.at[0], new_momentum_ref, sems.at[0]),
+        pltpu.make_async_copy(held.at[1], new_master_ref, sems.at[1]),
+    ]
+    for copy in pending:
+        copy.start()
     for m in range(2):
         exponents = widen(coded_ref[m, 256:272, :])
         for u in range(4):
@@ -138,10 +152,8 @@
             base = decode(far_ref[u, 272 + 64 * m : 336 + 64 * m, :], base_exponents[4 + m : 5 + m])
             grad = decode(coded_ref[m, 64 * u : 64 * u + 64, :], exponents[u : u + 1])
             blocks_ref[m, u] = (base - (0.7 * 1.9) * (grad * factor)).astype(jnp.bfloat16)
-    clipped = (grad_ref[mine_ref[0]] * factor).reshape(2, 32, 128)
-    new_momentum = 0.9 * momentum_ref[...] + clipped
-    new_momentum_ref[...] = new_momentum
-    new_master_ref[...] = master_ref[...] - 0.7 * (clipped + 0.9 * new_momentum)
+    for copy in pending:
+        copy.wait()
 
 
 def place_kernel(blocks_ref, out_ref, quarters, sems):
@@ -198,7 +210,8 @@
         "grad",
         [((4, 64, 128), f32), ((272, 128), i16), ((128, 1, 128), f32)],
         [VMEM] * 2,
-        [VMEM] * 3,
+        [VMEM, VMEM, HBM],
+        [pltpu.VMEM((128, 1, 128), f32), dma(())],
     )(total, far)
     parts = exchange(squares, ("x", "m", "p", "y", "c"))
     coded = lax.all_gather(coded, "m", axis=0)
@@ -207,7 +220,8 @@
         "update",
         [((2, 4, 64, 128), bf16), ((2, 32, 128), f32), ((2, 32, 128), f32)],
         [SMEM] + [VMEM] * 6,
-        [VMEM] * 3,
+        [VMEM, HBM, HBM],
+        [pltpu.VMEM((2, 2, 32, 128), f32), dma((2,))],
     )(mine, parts, far, coded, grad, master, momentum)
     blocks = exchange(copies(blocks, 8), ("x", "p"))
     (new_global,) = call(place_kernel, "place", [((2, 32, D), bf16)], [VMEM], [HBM], [held, dma((4,))])(blocks.reshape(8, 2, 4, 64, 128))

time: 103 us -> 104 us (level)
  no operation moved by 1% of the time
where the time goes in v7:
time: 104 us; the launch traced here: 103 us
  blocking collectives  69.2 us (67%)
  starting transfers between devices  20.4 us (20%)
  waiting for transfers between devices  6.83 us (7%)
  Pallas kernels  5.75 us (6%)
    all_to_all x2, blocking collectives, exchange(): return lax.all_to_all(blocks, axes, 0, 0, tiled=True)  28.7 us
    all_gather x1, blocking collectives, shards(): far = lax.all_gather(packed, 'u', axis=0)  25.5 us
    all_to_all x2, starting transfers between devices, exchange(): return lax.all_to_all(blocks, axes, 0, 0, tiled=True)  20.4 us
    all_gather x1, blocking collectives, shards(): bases = lax.all_gather(base, 'm', axis=0)  7.98 us
    all_gather x1, blocking collectives, shards(): coded = lax.all_gather(coded, 'm', axis=0)  7.05 us
    all_to_all x2, waiting for transfers between devices, exchange(): return lax.all_to_all(blocks, axes, 0, 0, tiled=True)  6.83 us
    pallas_call x1, Pallas kernels, shards(): call(term_kernel, 'term', [((8, 8, 2, 32, 128), bf16), ((8, 128), f32)],...  2.68 us
  transfers between devices with their start and end apart: 2, of which 2 were waited for; matrix products, arithmetic and copies ran while one was open for 0% of the time, Pallas kernels for 0%

profile of v7, /device:TPU:1, one launch (start us, length us, event | category | flops | bytes accessed | tf_op | source)
XLA Modules:
  0.0 103.1 jit_solution(16344528163576898330)
XLA Ops:
  0.6 2.7 %term.1 = (bf16[8,8,2,32,128]{4,3,2,1,0:T(8,128)(2,1)}, f32[8,128]{1,0:T(8,128)}) custom-call(s32[1]{0:T(128)} %bitcast.1.position_ref, s32[1,64]{1,0:T(1,128)} %bitcast.10, bf16[1,2,32,8192]{3,2,1,0:T(8,128)(2,1)} %anchor_ref.1, bf16[1,2,32,8192]{3,2,1,0:T(8,128)(2,1)} %local_ref.1), custom_call_target="tpu_custom_call" | custom-call | tf_op jit(solution)/shard_map/term/pallas_call | solution.py:190
  3.3 0.0 copy-start
  3.3 0.0 copy-start.1
  3.4 6.2 %all-to-all-start = ((bf16[8,8,2,32,128]{4,3,2,1,0:T(8,128)(2,1)}), bf16[8,8,2,32,128]{4,3,2,1,0:T(8,128)(2,1)S(1)}, u32[]{:S(2)}, u32[]{:S(2)}) async-start(bf16[8,8,2,32,128]{4,3,2,1,0:T(8,128)(2,1)} %get-tuple-element.14), calls=%async_computation | async-start | bytes 2097152 | tf_op jit(solution)/shard_map/all_to_all | solution.py:17
  9.6 0.0 copy-done
  9.6 0.0 copy-done.1
  9.6 8.0 %all-gather = s16[160,128]{1,0:T(8,128)(2,1)S(1)} all-gather(s16[80,128]{1,0:T(8,128)(2,1)S(1)} %base.1), channel_id=2, replica_groups=mesh['x'=4,'u'=4,'m'=2,'p'=2,'y'=4,'c'=2] {'m'}, dimensions={0}, use_global_device_ids=true | all-gather | bytes 61440 | tf_op jit(solution)/shard_map/all_gather | solution.py:201
  17.6 4.2 %all-to-all-done.near_ref = bf16[8,8,2,32,128]{4,3,2,1,0:T(8,128)(2,1)S(1)} async-done(((bf16[8,8,2,32,128]{4,3,2,1,0:T(8,128)(2,1)}), bf16[8,8,2,32,128]{4,3,2,1,0:T(8,128)(2,1)S(1)}, u32[]{:S(2)}, u32[]{:S(2)}) %all-to-all-start) | async-done | bytes 1048608 | tf_op jit(solution)/shard_map/all_to_all | solution.py:17
  21.8 0.2 near.1
  22.0 11.4 %all_to_all.20.coded_ref = s16[2,272,128]{2,1,0:T(8,128)(2,1)S(1)} all-to-all(s16[2,272,128]{2,1,0:T(8,128)(2,1)S(1)} %get-tuple-element.15), channel_id=1, replica_groups=mesh['x'=4,'u'=4,'m'=2,'p'=2,'y'=4,'c'=2] {'m'}, dimensions={0} | all-to-all | bytes 278528 | tf_op jit(solution)/shard_map/all_to_all | solution.py:17
  33.4 0.1 far.1
  33.5 0.0 copy-start.2
  33.5 25.5 %all-gather.1 = s16[1600,128]{1,0:T(8,128)(2,1)S(1)} all-gather(s16[400,128]{1,0:T(8,128)(2,1)S(1)} %far.1), channel_id=3, replica_groups=mesh['x'=4,'u'=4,'m'=2,'p'=2,'y'=4,'c'=2] {'u'}, dimensions={0}, use_global_device_ids=true | all-gather | bytes 512000 | tf_op jit(solution)/shard_map/all_gather | solution.py:207
  59.0 0.0 copy-done.2
  59.0 0.9 grad.1
  59.9 14.1 %all-to-all-start.2 = ((f32[128,1,128]{2,1,0:T(1,128)}), f32[128,1,128]{2,1,0:T(1,128)S(1)}, u32[]{:S(2)}, u32[]{:S(2)}) async-start(f32[128,1,128]{2,1,0:T(1,128)} %get-tuple-element.17), calls=%async_computation.2 | async-start | bytes 131072 | tf_op jit(solution)/shard_map/all_to_all | solution.py:17
  74.0 7.1 %all-gather.2 = s16[544,128]{1,0:T(8,128)(2,1)S(1)} all-gather(s16[272,128]{1,0:T(8,128)(2,1)S(1)} %get-tuple-element.18), channel_id=4, replica_groups=mesh['x'=4,'u'=4,'m'=2,'p'=2,'y'=4,'c'=2] {'m'}, dimensions={0}, use_global_device_ids=true | all-gather | bytes 208896 | tf_op jit(solution)/shard_map/all_gather | solution.py:217
  81.1 2.7 %all-to-all-done.2.parts_ref = f32[128,1,128]{2,1,0:T(1,128)S(1)} async-done(((f32[128,1,128]{2,1,0:T(1,128)}), f32[128,1,128]{2,1,0:T(1,128)S(1)}, u32[]{:S(2)}, u32[]{:S(2)}) %all-to-all-start.2) | async-done | bytes 65568 | tf_op jit(solution)/shard_map/all_to_all | solution.py:17
  83.7 0.8 update.1
  84.6 0.2 broadcast_in_dim.2
  84.8 17.3 %all_to_all.21.blocks_ref = bf16[8,2,4,64,128]{4,3,2,1,0:T(8,128)(2,1)S(1)} all-to-all(bf16[8,2,4,64,128]{4,3,2,1,0:T(8,128)(2,1)S(1)} %broadcast_in_dim.2), channel_id=1, replica_groups=mesh['x'=4,'u'=4,'m'=2,'p'=2,'y'=4,'c'=2] {'x','p'}, dimensions={0} | all-to-all | bytes 2097152 | tf_op jit(solution)/shard_map/all_to_all | solution.py:17
  102.1 1.0 %place.1 = bf16[2,32,8192]{2,1,0:T(8,128)(2,1)} custom-call(bf16[8,2,4,64,128]{4,3,2,1,0:T(8,128)(2,1)S(1)} %all_to_all.21.blocks_ref), custom_call_target="tpu_custom_call" | custom-call | tf_op jit(solution)/shard_map/place/pallas_call | solution.py:227
  (1 shorter events, 0.0 us)
Async XLA Ops:
  3.3 6.2 %copy-start = (f32[2,32,128]{2,1,0:T(8,128)S(1)}, f32[2,32,128]{2,1,0:T(8,128)}, u32[]{:S(2)}) copy-start(f32[2,32,128]{2,1,0:T(8,128)} %master_ref.3) | copy-start | bytes 98308
  3.3 6.2 %copy-start.1 = (f32[2,32,128]{2,1,0:T(8,128)S(1)}, f32[2,32,128]{2,1,0:T(8,128)}, u32[]{:S(2)}) copy-start(f32[2,32,128]{2,1,0:T(8,128)} %momentum_ref.3) | copy-start | bytes 98308
  3.4 18.4 %all-to-all-start = ((bf16[8,8,2,32,128]{4,3,2,1,0:T(8,128)(2,1)}), bf16[8,8,2,32,128]{4,3,2,1,0:T(8,128)(2,1)S(1)}, u32[]{:S(2)}, u32[]{:S(2)}) async-start(bf16[8,8,2,32,128]{4,3,2,1,0:T(8,128)(2,1)} %get-tuple-element.14), calls=%async_computation | async-start | bytes 2097152 | tf_op jit(solution)/shard_map/all_to_all | solution.py:17
  33.5 25.5 %copy-start.2 = (f32[8,128]{1,0:T(8,128)S(1)}, f32[8,128]{1,0:T(8,128)}, u32[]{:S(2)}) copy-start(f32[8,128]{1,0:T(8,128)} %get-tuple-element.13.total_ref) | copy-start | bytes 12292
  59.9 23.9 %all-to-all-start.2 = ((f32[128,1,128]{2,1,0:T(1,128)}), f32[128,1,128]{2,1,0:T(1,128)S(1)}, u32[]{:S(2)}, u32[]{:S(2)}) async-start(f32[128,1,128]{2,1,0:T(1,128)} %get-tuple-element.17), calls=%async_computation.2 | async-start | bytes 131072 | tf_op jit(solution)/shard_map/all_to_all | solution.py:17

commit v8 on v6

--- a/solution.py
+++ b/solution.py
@@ -127,10 +127,14 @@
     squares_ref[...] = jnp.broadcast_to(squares[None], (128, 1, 128))
 
 
-def update_kernel(mine_ref, parts_ref, far_ref, coded_ref, grad_ref, master_ref, momentum_ref, blocks_ref, new_master_ref, new_momentum_ref):
+def factor_of(parts_ref):
     norm = jnp.sqrt(jnp.sum(parts_ref[...], axis=0))
     limit = 0.001 * float(2 * ROWS * D) ** 0.5
-    factor = jnp.minimum(1.0, limit / (norm + 1e-06))
+    return jnp.minimum(1.0, limit / (norm + 1e-06))
+
+
+def update_kernel(parts_ref, far_ref, coded_ref, blocks_ref):
+    factor = factor_of(parts_ref)
     for m in range(2):
         exponents = widen(coded_ref[m, 256:272, :])
         for u in range(4):
@@ -138,19 +142,23 @@
             base = decode(far_ref[u, 272 + 64 * m : 336 + 64 * m, :], base_exponents[4 + m : 5 + m])
             grad = decode(coded_ref[m, 64 * u : 64 * u + 64, :], exponents[u : u + 1])
             blocks_ref[m, u] = (base - (0.7 * 1.9) * (grad * factor)).astype(jnp.bfloat16)
-    clipped = (grad_ref[mine_ref[0]] * factor).reshape(2, 32, 128)
-    new_momentum = 0.9 * momentum_ref[...] + clipped
-    new_momentum_ref[...] = new_momentum
-    new_master_ref[...] = master_ref[...] - 0.7 * (clipped + 0.9 * new_momentum)
-
-
-def place_kernel(blocks_ref, out_ref, quarters, sems):
+
+
+def place_kernel(mine_ref, blocks_ref, parts_ref, grad_ref, master_ref, momentum_ref, out_ref, new_master_ref, new_momentum_ref, quarters, held, sems, own_sems):
     pending = []
     for x in range(4):
         for z in range(16):
             block = blocks_ref[2 * x + z % 2, (z // 2) % 2, z // 4]
             quarters[x, :, :, 128 * z : 128 * z + 128] = block.reshape(2, 32, 128)
         copy = pltpu.make_async_copy(quarters.at[x], out_ref.at[:, :, pl.ds(2048 * x, 2048)], sems.at[x])
+        copy.start()
+        pending.append(copy)
+    clipped = (grad_ref[mine_ref[0]] * factor_of(parts_ref)).reshape(2, 32, 128)
+    new_momentum = 0.9 * momentum_ref[...] + clipped
+    held[0] = new_momentum
+    held[1] = master_ref[...] - 0.7 * (clipped + 0.9 * new_momentum)
+    for row, ref in enumerate((new_momentum_ref, new_master_ref)):
+        copy = pltpu.make_async_copy(held.at[row], ref, own_sems.at[row])
         copy.start()
         pending.append(copy)
     for copy in pending:
@@ -202,15 +210,17 @@
     )(total, far)
     parts = exchange(squares, ("x", "m", "p", "y", "c"))
     coded = lax.all_gather(coded, "m", axis=0)
-    blocks, new_master, new_momentum = call(
-        update_kernel,
-        "update",
-        [((2, 4, 64, 128), bf16), ((2, 32, 128), f32), ((2, 32, 128), f32)],
-        [SMEM] + [VMEM] * 6,
-        [VMEM] * 3,
-    )(mine, parts, far, coded, grad, master, momentum)
-    blocks = exchange(copies(blocks, 8), ("x", "p"))
-    (new_global,) = call(place_kernel, "place", [((2, 32, D), bf16)], [VMEM], [HBM], [held, dma((4,))])(blocks.reshape(8, 2, 4, 64, 128))
+    (blocks,) = call(update_kernel, "update", [((2, 4, 64, 128), bf16)], [VMEM] * 3, [VMEM])(parts, far, coded)
+    blocks = exchange(copies(blocks, 8), ("x", "p")).reshape(8, 2, 4, 64, 128)
+    block = ((2, 32, 128), f32)
+    new_global, new_master, new_momentum = call(
+        place_kernel,
+        "place",
+        [((2, 32, D), bf16), block, block],
+        [SMEM] + [VMEM] * 5,
+        [HBM] * 3,
+        [held, pltpu.VMEM((2, 2, 32, 128), f32), dma((4,)), dma((2,))],
+    )(mine, blocks, parts, grad, master, momentum)
     return (new_global, new_master, new_momentum)
 
 

time: 103 us -> 103 us (level)
  no operation moved by 1% of the time
where the time goes in v8:
time: 103 us
  blocking collectives  69.2 us (67%)
  starting transfers between devices  20.3 us (20%)
  waiting for transfers between devices  6.83 us (7%)
  Pallas kernels  5.16 us (5%)
    all_to_all x2, blocking collectives, exchange(): return lax.all_to_all(blocks, axes, 0, 0, tiled=True)  28.7 us
    all_gather x1, blocking collectives, shards(): far = lax.all_gather(packed, 'u', axis=0)  25.5 us
    all_to_all x2, starting transfers between devices, exchange(): return lax.all_to_all(blocks, axes, 0, 0, tiled=True)  20.3 us
    all_gather x1, blocking collectives, shards(): bases = lax.all_gather(base, 'm', axis=0)  7.98 us
    all_gather x1, blocking collectives, shards(): coded = lax.all_gather(coded, 'm', axis=0)  7.05 us
    all_to_all x2, waiting for transfers between devices, exchange(): return lax.all_to_all(blocks, axes, 0, 0, tiled=True)  6.83 us
    pallas_call x1, Pallas kernels, shards(): call(term_kernel, 'term', [((8, 8, 2, 32, 128), bf16), ((8, 128), f32)],...  2.68 us
  transfers between devices with their start and end apart: 2, of which 2 were waited for; matrix products, arithmetic and copies ran while one was open for 0% of the time, Pallas kernels for 0%

profile of v8, /device:TPU:1, one launch (start us, length us, event | category | flops | bytes accessed | tf_op | source)
XLA Modules:
  0.0 102.5 jit_solution(4632035999178150112)
XLA Ops:
  0.6 2.7 %term.1 = (bf16[8,8,2,32,128]{4,3,2,1,0:T(8,128)(2,1)}, f32[8,128]{1,0:T(8,128)}) custom-call(s32[1]{0:T(128)} %bitcast.1.position_ref, s32[1,64]{1,0:T(1,128)} %bitcast.10, bf16[1,2,32,8192]{3,2,1,0:T(8,128)(2,1)} %anchor_ref.1, bf16[1,2,32,8192]{3,2,1,0:T(8,128)(2,1)} %local_ref.1), custom_call_target="tpu_custom_call" | custom-call | tf_op jit(solution)/shard_map/term/pallas_call | solution.py:186
  3.3 0.0 copy-start
  3.3 0.0 copy-start.1
  3.4 6.2 %all-to-all-start = ((bf16[8,8,2,32,128]{4,3,2,1,0:T(8,128)(2,1)}), bf16[8,8,2,32,128]{4,3,2,1,0:T(8,128)(2,1)S(1)}, u32[]{:S(2)}, u32[]{:S(2)}) async-start(bf16[8,8,2,32,128]{4,3,2,1,0:T(8,128)(2,1)} %get-tuple-element.11), calls=%async_computation | async-start | bytes 2097152 | tf_op jit(solution)/shard_map/all_to_all | solution.py:17
  9.6 0.0 copy-done
  9.6 0.0 copy-done.1
  9.6 8.0 %all-gather = s16[160,128]{1,0:T(8,128)(2,1)S(1)} all-gather(s16[80,128]{1,0:T(8,128)(2,1)S(1)} %base.1), channel_id=2, replica_groups=mesh['x'=4,'u'=4,'m'=2,'p'=2,'y'=4,'c'=2] {'m'}, dimensions={0}, use_global_device_ids=true | all-gather | bytes 61440 | tf_op jit(solution)/shard_map/all_gather | solution.py:197
  17.6 4.2 %all-to-all-done.near_ref = bf16[8,8,2,32,128]{4,3,2,1,0:T(8,128)(2,1)S(1)} async-done(((bf16[8,8,2,32,128]{4,3,2,1,0:T(8,128)(2,1)}), bf16[8,8,2,32,128]{4,3,2,1,0:T(8,128)(2,1)S(1)}, u32[]{:S(2)}, u32[]{:S(2)}) %all-to-all-start) | async-done | bytes 1048608 | tf_op jit(solution)/shard_map/all_to_all | solution.py:17
  21.8 0.2 near.1
  22.0 11.4 %all_to_all.20.coded_ref = s16[2,272,128]{2,1,0:T(8,128)(2,1)S(1)} all-to-all(s16[2,272,128]{2,1,0:T(8,128)(2,1)S(1)} %get-tuple-element.12), channel_id=1, replica_groups=mesh['x'=4,'u'=4,'m'=2,'p'=2,'y'=4,'c'=2] {'m'}, dimensions={0} | all-to-all | bytes 278528 | tf_op jit(solution)/shard_map/all_to_all | solution.py:17
  33.4 0.1 far.1
  33.5 0.0 copy-start.2
  33.5 25.5 %all-gather.1 = s16[1600,128]{1,0:T(8,128)(2,1)S(1)} all-gather(s16[400,128]{1,0:T(8,128)(2,1)S(1)} %far.1), channel_id=3, replica_groups=mesh['x'=4,'u'=4,'m'=2,'p'=2,'y'=4,'c'=2] {'u'}, dimensions={0}, use_global_device_ids=true | all-gather | bytes 512000 | tf_op jit(solution)/shard_map/all_gather | solution.py:203
  59.0 0.0 copy-done.2
  59.0 0.9 grad.1
  59.9 14.1 %all-to-all-start.2 = ((f32[128,1,128]{2,1,0:T(1,128)}), f32[128,1,128]{2,1,0:T(1,128)S(1)}, u32[]{:S(2)}, u32[]{:S(2)}) async-start(f32[128,1,128]{2,1,0:T(1,128)} %get-tuple-element.14), calls=%async_computation.2 | async-start | bytes 131072 | tf_op jit(solution)/shard_map/all_to_all | solution.py:17
  74.0 7.1 %all-gather.2 = s16[544,128]{1,0:T(8,128)(2,1)S(1)} all-gather(s16[272,128]{1,0:T(8,128)(2,1)S(1)} %get-tuple-element.15), channel_id=4, replica_groups=mesh['x'=4,'u'=4,'m'=2,'p'=2,'y'=4,'c'=2] {'m'}, dimensions={0}, use_global_device_ids=true | all-gather | bytes 208896 | tf_op jit(solution)/shard_map/all_gather | solution.py:212
  81.1 2.7 %all-to-all-done.2.parts_ref = f32[128,1,128]{2,1,0:T(1,128)S(1)} async-done(((f32[128,1,128]{2,1,0:T(1,128)}), f32[128,1,128]{2,1,0:T(1,128)S(1)}, u32[]{:S(2)}, u32[]{:S(2)}) %all-to-all-start.2) | async-done | bytes 65568 | tf_op jit(solution)/shard_map/all_to_all | solution.py:17
  83.7 0.2 update.1
  83.9 0.2 broadcast_in_dim.2
  84.2 17.3 %all_to_all.21.blocks_ref = bf16[8,2,4,64,128]{4,3,2,1,0:T(8,128)(2,1)S(1)} all-to-all(bf16[8,2,4,64,128]{4,3,2,1,0:T(8,128)(2,1)S(1)} %broadcast_in_dim.2), channel_id=1, replica_groups=mesh['x'=4,'u'=4,'m'=2,'p'=2,'y'=4,'c'=2] {'x','p'}, dimensions={0} | all-to-all | bytes 2097152 | tf_op jit(solution)/shard_map/all_to_all | solution.py:17
  101.5 1.1 %place.1 = (bf16[2,32,8192]{2,1,0:T(8,128)(2,1)}, f32[2,32,128]{2,1,0:T(8,128)}, f32[2,32,128]{2,1,0:T(8,128)}) custom-call(s32[1]{0:T(128)} %bitcast.mine_ref, bf16[8,2,4,64,128]{4,3,2,1,0:T(8,128)(2,1)S(1)} %all_to_all.21.blocks_ref, f32[128,1,128]{2,1,0:T(1,128)S(1)} %all-to-all-done.2.parts_ref, f32[4,64,128]{2,1,0:T(8,128)S(1)} %get-tuple-element.16.grad_ref, ...), custom_call_target="tpu_custom_call" | custom-call | tf_op jit(solution)/shard_map/place/pallas_call | solution.py:216
  (1 shorter events, 0.0 us)
Async XLA Ops:
  3.3 6.2 %copy-start = (f32[2,32,128]{2,1,0:T(8,128)S(1)}, f32[2,32,128]{2,1,0:T(8,128)}, u32[]{:S(2)}) copy-start(f32[2,32,128]{2,1,0:T(8,128)} %master_ref.3) | copy-start | bytes 98308
  3.3 6.2 %copy-start.1 = (f32[2,32,128]{2,1,0:T(8,128)S(1)}, f32[2,32,128]{2,1,0:T(8,128)}, u32[]{:S(2)}) copy-start(f32[2,32,128]{2,1,0:T(8,128)} %momentum_ref.3) | copy-start | bytes 98308
  3.4 18.4 %all-to-all-start = ((bf16[8,8,2,32,128]{4,3,2,1,0:T(8,128)(2,1)}), bf16[8,8,2,32,128]{4,3,2,1,0:T(8,128)(2,1)S(1)}, u32[]{:S(2)}, u32[]{:S(2)}) async-start(bf16[8,8,2,32,128]{4,3,2,1,0:T(8,128)(2,1)} %get-tuple-element.11), calls=%async_computation | async-start | bytes 2097152 | tf_op jit(solution)/shard_map/all_to_all | solution.py:17
  33.5 25.5 %copy-start.2 = (f32[8,128]{1,0:T(8,128)S(1)}, f32[8,128]{1,0:T(8,128)}, u32[]{:S(2)}) copy-start(f32[8,128]{1,0:T(8,128)} %get-tuple-element.10.total_ref) | copy-start | bytes 12292
  59.9 23.8 %all-to-all-start.2 = ((f32[128,1,128]{2,1,0:T(1,128)}), f32[128,1,128]{2,1,0:T(1,128)S(1)}, u32[]{:S(2)}, u32[]{:S(2)}) async-start(f32[128,1,128]{2,1,0:T(1,128)} %get-tuple-element.14), calls=%async_computation.2 | async-start | bytes 131072 | tf_op jit(solution)/shard_map/all_to_all | solution.py:17
